TPU v7x, 256 devices: a whole 4x4x8 slice. The times are simulated.
256 devices in a mesh: grp: 4 (over x), lay: 64 (over y, z, core).
Axes of the slice: x: 4, y: 4, z: 8, core: 2. Of those that a mesh axis runs over, the one named last changes fastest.
Arguments:
- weights: bfloat16 [512, 1024, 1024], P(('grp', 'lay')), may hold values from -0.1875 to 0.1875
- biases: float32 [512, 1024], P(('grp', 'lay')), may hold values from -3 to 3
- states: bfloat16 [512, 128, 1024], P(('grp', 'lay')), may hold values from -6 to 6
- guess: float32 [256, 128, 1024], P(('grp', 'lay')), may hold values from -6 to 6
- output_grad: float32 [128, 1024], replicated, may hold values from -6 to 6
- coarse_rate: float32 [256, 1024], P(('grp', 'lay')), may hold values from 0 to 1, as said below
Outputs:
- corrected: float32 [256, 128, 1024], P(('grp', 'lay'))
- weight_grads: bfloat16 [512, 1024, 1024], P(('grp', 'lay'))
- residual: float32 [256, 128, 1024], P(('grp', 'lay'))
Inputs may be any that keep to these rules, and one draw needn't show every extreme that they name: `coarse_rate`: every entry is positive.
All inputs are finite; a program needn't handle non-finite values.
Results may differ from a plain program's by a relative error of at most 0.0085.
Values sent between devices are 32-bit elements; how exact they have to be, the bound alone decides.
No kernel may reach another device: no remote copies, remote signals or barrier semaphores. Data moves between devices by JAX's collectives and lax.ppermute only.
A program may use at most 320 MiB of HBM per device.

v0:
```python
import jax
import jax.numpy as jnp
from jax import lax
from jax.sharding import PartitionSpec as P


def shifted(array, axis, by):
    devices = lax.axis_size(axis)
    pairs = [(i, i + by) for i in range(devices) if 0 <= i + by < devices]
    return lax.ppermute(array, axis, pairs)


def prefix(part, axis, combine, identity):
    count = lax.axis_size(axis)
    place = lax.axis_index(axis)
    ahead = count - 1 - place
    gathered = jax.tree.map(lambda a: lax.all_gather(a, axis), part)
    state = jax.tree.map(lambda a, e: jnp.zeros_like(a) + jnp.asarray(e, a.dtype), part, identity)

    def one(lap, state):
        source = count - 1 - lap
        return combine(
            state, jax.tree.map(lambda a: lax.dynamic_index_in_dim(a, source, 0, False), gathered)
        )

    return lax.fori_loop(0, ahead, one, state)


def broadcast(block, axis, holder):
    block = jnp.where(lax.axis_index(axis) == holder, block, jnp.zeros_like(block))
    return lax.psum(block, axis)


def layer_slopes(weights, biases, states):
    slopes = []
    for k in range(weights.shape[0]):
        pre = (
            jnp.dot(states[k], weights[k], preferred_element_type=jnp.float32) + biases[k][None, :]
        )
        act = jnp.tanh(pre)
        slopes.append(1.0 - act * act)
    return slopes


def sweep(lam, slopes, weights, states, keep):
    count = weights.shape[0]
    batch = states.shape[1]
    grads = []
    for k in reversed(range(count)):
        q = (lam * slopes[k]).astype(jnp.bfloat16)
        if keep:
            g = jnp.einsum("bi,bj->ij", states[k], q, preferred_element_type=jnp.float32) * (
                0.5 / batch
            )
            grads.append(g.astype(jnp.bfloat16))
        lam = lam + 0.5 * jnp.einsum("bj,ij->bi", q, weights[k], preferred_element_type=jnp.float32)
    if keep:
        return jnp.stack(grads[::-1])
    return lam


def compose(preceding_step, later):
    return (later[0] * preceding_step[0], later[0] * preceding_step[1] + later[1])


def on_device(weights, biases, states, guess, output_grad, coarse_rate):
    slopes = layer_slopes(weights, biases, states)
    is_top = lax.axis_index(("grp", "lay")) == lax.axis_size(("grp", "lay")) - 1
    start = guess[0]
    moved = sweep(start, slopes, weights, states, False)
    above = shifted(moved, ("grp", "lay"), -1)
    first = jnp.where(is_top, start, above)
    moved2 = sweep(first, slopes, weights, states, False)
    upper_second = shifted(moved2, ("grp", "lay"), -1)
    residual = jnp.where(is_top, output_grad - first, upper_second - first)
    multiplier_coefficient = jnp.exp(-coarse_rate)
    own = (multiplier_coefficient, residual)
    identity_matrix = (jnp.ones_like(multiplier_coefficient), jnp.zeros_like(residual))
    inner = prefix(own, "lay", compose, identity_matrix)
    whole = compose(inner, own)
    spread = (broadcast(whole[0], "lay", 0), broadcast(whole[1], "lay", 0))
    outer = prefix(spread, "grp", compose, identity_matrix)
    total = compose(outer, inner)
    err = multiplier_coefficient * total[1] + residual
    corrected = first + err
    grads = sweep(corrected, slopes, weights, states, True)
    return (corrected[None], grads, residual[None])


def solution(mesh):
    placed = (
        P(("grp", "lay"), None, None),
        P(("grp", "lay"), None),
        P(("grp", "lay"), None, None),
        P(("grp", "lay"), None, None),
        P(),
        P(("grp", "lay"), None),
    )
    return jax.shard_map(
        on_device,
        mesh=mesh,
        in_specs=placed,
        out_specs=(
            P(("grp", "lay"), None, None),
            P(("grp", "lay"), None, None),
            P(("grp", "lay"), None, None),
        ),
        check_vma=False,
    )
```

profile of v0, /device:TPU:1, one launch (start us, length us, event | category | flops | bytes accessed | tf_op | source)
XLA Modules:
  0.0 610.7 jit_solution(3297037519489694577)
XLA Ops:
  8.1 2.6 fusion.32
  10.7 2.2 fusion.65
  14.6 5.2 collective-permute-start
  19.8 6.6 %collective-permute-done = f32[128,1024]{1,0:T(8,128)S(1)} collective-permute-done((f32[128,1024]{1,0:T(8,128)S(1)}, f32[128,1024]{1,0:T(8,128)S(1)}, u32[]{:S(2)}, u32[]{:S(2)}) %collective-permute-start) | collective-permute-done | bytes 524320 | tf_op jit(solution)/shard_map/ppermute | solution.py:10
  26.5 2.4 fusion.44
  29.8 1.9 collective-permute-start.1
  31.7 8.6 %collective-permute-done.1 = f32[128,1024]{1,0:T(8,128)S(1)} collective-permute-done((f32[128,1024]{1,0:T(8,128)S(1)}, f32[128,1024]{1,0:T(8,128)S(1)}, u32[]{:S(2)}, u32[]{:S(2)}) %collective-permute-start.1) | collective-permute-done | bytes 524320 | tf_op jit(solution)/shard_map/ppermute | solution.py:10
  41.3 54.9 %all-gather.2 = f32[64,1,1024]{2,1,0:T(1,128)S(1)} all-gather(f32[1,1,1024]{2,1,0:T(1,128)S(1)} %get-tuple-element.204), channel_id=2, replica_groups=mesh['grp'=4,'lay'=64] {'lay'}, dimensions={0}, use_global_device_ids=true | all-gather | bytes 266240 | tf_op jit(solution)/shard_map/all_gather | solution.py:17
  96.3 96.9 %all-gather.8.cloned.1.call-done = f32[8192,1024]{1,0:T(8,128)} async-done(((f32[128,1024]{1,0:T(8,128)}), f32[8192,1024]{1,0:T(8,128)}) %all-gather.8.cloned.1.call-update) | async-done | bytes 33554448 | tf_op jit(solution)/shard_map/all_gather | solution.py:17
  193.2 80.9 %while.28 = (s32[]{:T(128)}, f32[1,1024]{1,0:T(1,128)S(1)}, f32[128,1024]{1,0:T(8,128)S(1)}, s32[]{:T(128)}, f32[64,1,1024]{2,1,0:T(1,128)S(1)}, /*index=5*/f32[...) while((s32[]{:T(128)}, f32[1,1024]{1,0:T(1,128)S(1)}, f32[128,1024]{1,0:T(8,128)S(1)}, ...), condition=%wide.region_1.2_spmd, body=%wide.region_0.1_spmd.sunk | while | flops 263174 | bytes 1593499 | solution.py:26
  193.3 1.3 bitcast_add_fusion.4
  194.6 1.3 bitcast_add_fusion.4
  195.9 1.3 bitcast_add_fusion.4
  197.2 1.3 bitcast_add_fusion.4
  198.6 1.3 bitcast_add_fusion.4
  199.9 1.3 bitcast_add_fusion.4
  201.2 1.3 bitcast_add_fusion.4
  202.5 1.3 bitcast_add_fusion.4
  203.8 1.3 bitcast_add_fusion.4
  205.1 1.3 bitcast_add_fusion.4
  206.4 1.3 bitcast_add_fusion.4
  207.7 1.3 bitcast_add_fusion.4
  209.0 1.3 bitcast_add_fusion.4
  210.3 1.3 bitcast_add_fusion.4
  211.6 1.3 bitcast_add_fusion.4
  212.9 1.3 bitcast_add_fusion.4
  214.2 1.3 bitcast_add_fusion.4
  215.5 1.3 bitcast_add_fusion.4
  216.8 1.3 bitcast_add_fusion.4
  218.1 1.3 bitcast_add_fusion.4
  219.4 1.3 bitcast_add_fusion.4
  220.7 1.3 bitcast_add_fusion.4
  222.0 1.3 bitcast_add_fusion.4
  223.3 1.3 bitcast_add_fusion.4
  224.6 1.3 bitcast_add_fusion.4
  225.9 1.3 bitcast_add_fusion.4
  227.2 1.3 bitcast_add_fusion.4
  228.5 1.3 bitcast_add_fusion.4
  229.9 1.3 bitcast_add_fusion.4
  231.2 1.3 bitcast_add_fusion.4
  232.5 1.3 bitcast_add_fusion.4
  233.8 1.3 bitcast_add_fusion.4
  235.1 1.3 bitcast_add_fusion.4
  236.4 1.3 bitcast_add_fusion.4
  237.7 1.3 bitcast_add_fusion.4
  239.0 1.3 bitcast_add_fusion.4
  240.3 1.3 bitcast_add_fusion.4
  241.6 1.3 bitcast_add_fusion.4
  242.9 1.3 bitcast_add_fusion.4
  244.2 1.3 bitcast_add_fusion.4
  245.5 1.3 bitcast_add_fusion.4
  246.8 1.3 bitcast_add_fusion.4
  248.1 1.3 bitcast_add_fusion.4
  249.4 1.3 bitcast_add_fusion.4
  250.7 1.3 bitcast_add_fusion.4
  253.3 1.3 bitcast_add_fusion.4
  255.9 1.3 bitcast_add_fusion.4
  275.1 174.0 %all-reduce.2.cloned.1.call-done = f32[1,128,1024]{2,1,0:T(8,128)} async-done(((f32[1,128,1024]{2,1,0:T(8,128)}), f32[1,128,1024]{2,1,0:T(8,128)}) %all-reduce.2.cloned.1.call-update) | async-done | bytes 524304 | tf_op jit(solution)/shard_map/psum | solution.py:31
  449.2 125.9 %psum.14 = f32[1,1,1024]{2,1,0:T(1,128)S(1)} all-reduce(f32[1,1,1024]{2,1,0:T(1,128)S(1)} %fusion.96), channel_id=1, replica_groups=mesh['grp'=4,'lay'=64] {'lay'}, use_global_device_ids=true, to_apply=%region_2.3 | all-reduce | flops 1024 | bytes 8192 | tf_op jit(solution)/shard_map/psum | solution.py:31
  575.1 9.3 %all_gather.29 = f32[4,1,1024]{2,1,0:T(1,128)S(1)} all-gather(f32[1,1,1024]{2,1,0:T(1,128)S(1)} %psum.14), channel_id=1, replica_groups=mesh['grp'=4,'lay'=64] {'grp'}, dimensions={0}, use_global_device_ids=true | all-gather | bytes 20480 | tf_op jit(solution)/shard_map/all_gather | solution.py:17
  584.5 3.9 while.29
  589.3 4.7 fusion.14
  595.7 2.3 pad_maximum_fusion
  598.0 6.2 %copy.10 = bf16[2,1024,1024]{2,1,0:T(8,128)(2,1)} copy(bf16[2,1024,1024]{1,2,0:T(8,128)(2,1)} %pad_maximum_fusion) | data formatting | bytes 8388608
  (122 shorter events, 31.9 us)
Async XLA Ops:
  7.2 5.7 copy-start.5
  7.2 186.0 %all-gather.8.cloned.1.call-start = ((), (), s32[]{:S(2)}) async-start(), calls=%async_computation.2 | async-start | bytes 34078720 | tf_op jit(solution)/shard_map/all_gather | solution.py:17
  7.2 5.7 copy-start
  14.6 11.8 %collective-permute-start = (f32[128,1024]{1,0:T(8,128)S(1)}, f32[128,1024]{1,0:T(8,128)S(1)}, u32[]{:S(2)}, u32[]{:S(2)}) collective-permute-start(f32[128,1024]{1,0:T(8,128)S(1)} %fusion.71), channel_id=1, source_target_pairs={{1,0},{2,1},{3,2},{4,3},{5,4},{6,5},{7,6},{8,7},{9,8},{10,9},{11,1... | collective-permute-start | bytes 1572872 | tf_op jit(solution)/shard_map/ppermute | solution.py:10
  19.8 9.1 %copy-start.1 = (bf16[2,1024,1024]{2,1,0:T(8,128)(2,1)S(1)}, bf16[2,1024,1024]{2,1,0:T(8,128)(2,1)}, u32[]{:S(2)}) copy-start(bf16[2,1024,1024]{2,1,0:T(8,128)(2,1)} %param.10) | copy-start | bytes 12582916
  19.8 20.5 %copy-start.6 = (f32[128,1024]{1,0:T(8,128)S(1)}, f32[128,1024]{1,0:T(8,128)}, u32[]{:S(2)}) copy-start(f32[128,1024]{1,0:T(8,128)} %param.14) | copy-start | bytes 1572868
  26.5 14.8 %copy-start.8 = (f32[1,1024]{1,0:T(1,128)S(1)}, f32[1,1024]{1,0:T(1,128)}, u32[]{:S(2)}) copy-start(f32[1,1024]{1,0:T(1,128)} %param.15) | copy-start | bytes 12292
  29.8 10.5 %collective-permute-start.1 = (f32[128,1024]{1,0:T(8,128)S(1)}, f32[128,1024]{1,0:T(8,128)S(1)}, u32[]{:S(2)}, u32[]{:S(2)}) collective-permute-start(f32[128,1024]{1,0:T(8,128)S(1)} %fusion.77), channel_id=1, source_target_pairs={{1,0},{2,1},{3,2},{4,3},{5,4},{6,5},{7,6},{8,7},{9,8},{10,9},{11,1... | collective-permute-start | bytes 1572872 | tf_op jit(solution)/shard_map/ppermute | solution.py:10
  41.3 407.9 %all-reduce.2.cloned.1.call-start = ((), (), s32[]{:S(2)}) async-start(), calls=%async_computation | async-start | bytes 1048576 | tf_op jit(solution)/shard_map/psum | solution.py:31
  193.2 80.9 %copy-start.2 = (f32[128,1024]{1,0:T(8,128)S(1)}, f32[128,1024]{1,0:T(8,128)}, u32[]{:S(2)}) copy-start(f32[128,1024]{1,0:T(8,128)} %subtract_select_fusion) | copy-start | bytes 1572868
  275.1 309.3 %all-gather.6.cloned.1.call-start = ((), (), s32[]{:S(2)}) async-start(), calls=%async_computation.1 | async-start | bytes 2621440 | tf_op jit(solution)/shard_map/all_gather | solution.py:17
  589.3 4.7 copy-start.4
  589.3 4.7 copy-start.7
  594.1 1.6 copy-start.3
Sparse Core Ops, SparseCore 0:
  41.4 151.7 all-gather.7
  275.2 173.9 all-reduce.1
  451.0 32.6 all-gather.5
where the time goes:
time: 616 us; the launch traced here: 611 us
  waiting for transfers between devices  286 us (46%)
  blocking collectives  190 us (31%)
  other arithmetic  87.9 us (14%)
  matrix products  15.2 us (2%)
  between operations  14 us (2%)
  local copies, waits for them, and re-layouts  8.06 us (1%)
  starting transfers between devices  7.19 us (1%)
    psum x1, waiting for transfers between devices, broadcast(): return lax.psum(block, axis)  174 us
    psum x1, blocking collectives, broadcast(): return lax.psum(block, axis)  126 us
    all_gather x2, waiting for transfers between devices, prefix(): gathered = jax.tree.map(lambda a: lax.all_gather(a, axis), part)  96.9 us
    add x65, other arithmetic, compose(): later[0] * preceding_step[1] + later[1]  81.6 us
    all_gather x2, blocking collectives, prefix(): gathered = jax.tree.map(lambda a: lax.all_gather(a, axis), part)  64.3 us
    ppermute x2, waiting for transfers between devices, shifted(): return lax.ppermute(array, axis, pairs)  15.2 us
  transfers between devices with their start and end apart: 5, of which 4 were waited for; matrix products, arithmetic and copies ran while one was open for 0% of the time, Pallas kernels for 0%

commit v1 on v0

v1 whole, which is shorter than its diff:
```python
import functools

import jax
import jax.numpy as jnp
from jax import lax
from jax.experimental import pallas as pl
from jax.experimental.pallas import tpu as pltpu
from jax.sharding import Mesh, PartitionSpec as P

ALL = ("x", "y", "z", "c")
PLANE = ("y", "z")
MIB = 1024 * 1024
F32 = jnp.float32
BF16 = jnp.bfloat16
HBM = pl.BlockSpec(memory_space=pl.ANY)
VMEM = pl.BlockSpec(memory_space=pltpu.VMEM)
COLS = 512
PART = 256
ROWS = 16
PIECE = ROWS + 1
LANES = 128


def params(mib):
    return pltpu.CompilerParams(vmem_limit_bytes=mib * MIB)


def in_vmem(x):
    return pltpu.with_memory_space_constraint(x, pltpu.VMEM)


def in_hbm(x):
    return pltpu.with_memory_space_constraint(x, pltpu.HBM)


def is_top():
    top = None
    for axis in ALL:
        last = lax.axis_index(axis) == lax.axis_size(axis) - 1
        top = last if top is None else jnp.logical_and(top, last)
    return top


def times(a, b):
    return jnp.dot(a, b, preferred_element_type=F32)


def times_transposed(a, b):
    return lax.dot_general(a, b, (((1,), (1,)), ((), ())), preferred_element_type=F32)


def transposed_times(a, b):
    return lax.dot_general(a, b, (((0,), (0,)), ((), ())), preferred_element_type=F32)


def first_kernel(w, b, s, g, moved, slopes, wv, sv, gv, bv, qv, wsem, sem):
    layers, width = wv.shape[0], wv.shape[2]
    parts = width // COLS
    order = list(reversed(range(layers)))

    def chunk(l, n):
        cols = pl.ds(n * COLS, COLS)
        return pltpu.make_async_copy(w.at[l, :, cols], wv.at[l, :, cols], wsem.at[l, n])

    states = [pltpu.make_async_copy(s.at[l], sv.at[l], sem.at[l]) for l in range(layers)]
    bias = pltpu.make_async_copy(b, bv, sem.at[layers])
    guess = pltpu.make_async_copy(g.at[0], gv, sem.at[layers + 1])
    for l in order:
        states[l].start()
        for n in range(parts):
            chunk(l, n).start()
            if l == order[0] and n == 0:
                bias.start()
                guess.start()
    bias.wait()
    lam = None
    for l in order:
        states[l].wait()
        for n in range(parts):
            cols = slice(n * COLS, (n + 1) * COLS)
            chunk(l, n).wait()
            act = jnp.tanh(times(sv[l], wv[l, :, cols]) + bv[l : l + 1, cols])
            slope = 1.0 - act * act
            slopes[l, :, cols] = slope
            if lam is None:
                guess.wait()
                lam = gv
            qv[l, :, cols] = (lam[:, cols] * slope).astype(BF16)
        moved[...] = lam[...] + 0.5 * times_transposed(qv[l], wv[l])
        lam = moved


def relax(lam, slopes, wv):
    for l in reversed(range(slopes.shape[0])):
        q = (lam * slopes[l]).astype(BF16)
        lam = lam + 0.5 * times_transposed(q, wv[l])
    return lam


def second_kernel(g, og, above, rup, moved, slopes, wv, first, res, keep, send, rest, lam, extra, sem):
    top = is_top()
    half = keep.shape[1]
    batch = lam.shape[0]

    @pl.when(top)
    def _():
        one = pltpu.make_async_copy(g.at[0], lam, sem.at[0])
        two = pltpu.make_async_copy(og, extra, sem.at[1])
        one.start()
        two.start()
        one.wait()
        two.wait()
        extra[...] = extra[...] - lam[...]

    @pl.when(jnp.logical_not(top))
    def _():
        lam[...] = above[...]
        extra[...] = jnp.zeros_like(extra)

    kept = pltpu.make_async_copy(lam, first, sem.at[0])
    kept.start()
    r = relax(lam[...], slopes, wv) - moved[...]
    res[...] = r
    f = jnp.exp(-rup[...])
    v = r + f * extra[...]
    low, high = v[:, :half], v[:, half:]
    core0 = lax.axis_index("c") == 0
    keep[...] = jnp.where(core0, low, high)
    send[:batch, :] = jnp.where(core0, high, low)
    send[batch:, :] = jnp.broadcast_to(
        jnp.where(core0, f[:, half:], f[:, :half]), (send.shape[0] - batch, half)
    )
    rest[...] = high
    kept.wait()


def chip_kernel(keep, got, rate, rup, out):
    batch, half = keep.shape
    core0 = lax.axis_index("c") == 0
    own, up = jnp.exp(-rate[...]), jnp.exp(-rup[...])
    below = jnp.where(core0, up[:, :half], got[batch : batch + 1, :])
    above = jnp.where(core0, own[:, :half], up[:, half:])
    kept, other = keep[...], got[:batch, :]
    total = jnp.where(core0, kept, other) + below * jnp.where(core0, other, kept)
    factor = below * above
    blocks = half // LANES
    for j in range(out.shape[0] // PIECE):
        r, n = j // blocks, j % blocks
        cols = slice(n * LANES, (n + 1) * LANES)
        out[PIECE * j : PIECE * j + ROWS, :] = total[r * ROWS : (r + 1) * ROWS, cols]
        out[PIECE * j + ROWS : PIECE * j + PIECE, :] = factor[:, cols]


def piece(got, j):
    return got[PIECE * j : PIECE * j + ROWS, :], got[PIECE * j + ROWS : PIECE * j + PIECE, :]


def plane_kernel(got, out):
    count = got.shape[0] // PIECE
    t, f = piece(got, count - 1)
    for j in reversed(range(count - 1)):
        tj, fj = piece(got, j)
        t = tj + fj * t
        f = fj * f
    out[:ROWS, :] = t
    out[ROWS:, :] = jnp.broadcast_to(f, (8, LANES))


def scan_kernel(got, one, two, three, res, rest, out):
    del res, rest
    place, size = lax.axis_index("x"), lax.axis_size("x")
    carry = jnp.zeros((ROWS, LANES), F32)
    for k, b in ((3, three), (2, two), (1, one)):
        t, f = b[:ROWS, :], b[ROWS : ROWS + 1, :]
        carry = jnp.where(place + k < size, t + f * carry, carry)
    for j in reversed(range(out.shape[0])):
        out[j, :, :] = carry
        if j:
            t, f = piece(got, j)
            carry = t + f * carry


def fetch_kernel(first, w, s, after, first_v, wv, sv, sem):
    del after
    copies = [
        pltpu.make_async_copy(first, first_v, sem.at[0]),
        pltpu.make_async_copy(s, sv, sem.at[1]),
        pltpu.make_async_copy(w.at[pl.ds(1, wv.shape[0])], wv, sem.at[2]),
    ]
    for copy in copies:
        copy.start()
    for copy in copies:
        copy.wait()


def final_kernel(
    q_own, q_other, got, rest, rate, slopes, first, wv, sv, og, res_in,
    corrected, grads, res, lam_v, err_v, extra, gbuf, sem, gsem,
):
    top = is_top()
    core0 = lax.axis_index("c") == 0
    batch, width = lam_v.shape
    half = width // 2
    blocks = half // LANES
    layers = slopes.shape[0]

    @pl.when(top)
    def _():
        one = pltpu.make_async_copy(og, extra, sem.at[3])
        one.start()
        one.wait()

    @pl.when(top)
    def _():
        extra[...] = extra[...] - first[...]
        pltpu.make_async_copy(extra, res.at[0], sem.at[3]).start()

    @pl.when(jnp.logical_not(top))
    def _():
        extra[...] = jnp.zeros_like(extra)
        pltpu.make_async_copy(res_in, res.at[0], sem.at[3]).start()

    f = jnp.exp(-rate[...])
    for j in range(q_own.shape[0]):
        r, n = j // blocks, j % blocks
        rows = slice(r * ROWS, (r + 1) * ROWS)
        for h in range(2):
            cols = slice(h * half + n * LANES, h * half + (n + 1) * LANES)
            e = jnp.where(core0 == (h == 0), q_own[j], q_other[j])
            lower = (got, rest)[h][rows, n * LANES : (n + 1) * LANES]
            err = jnp.where(core0, f[:, cols] * e + lower, e + extra[rows, cols])
            err_v[rows, cols] = err

    lam = first[...] + err_v[...]
    lam_v[...] = lam
    keep = pltpu.make_async_copy(lam_v, corrected.at[0], sem.at[0])
    keep.start()
    parts = width // PART
    copies = []
    for l in reversed(range(layers)):
        q = (lam * slopes[l]).astype(BF16)
        for n in range(parts):
            rows = slice(n * PART, (n + 1) * PART)
            out = transposed_times(sv[l, :, rows], q) * (0.5 / batch)
            gbuf[l, rows, :] = out.astype(BF16)
            there = grads.at[l, pl.ds(n * PART, PART)]
            copy = pltpu.make_async_copy(gbuf.at[l, pl.ds(n * PART, PART)], there, gsem.at[l, n])
            copy.start()
            copies.append(copy)
        if l:
            lam = lam + 0.5 * times_transposed(q, wv[l - 1])
    keep.wait()
    pltpu.make_async_copy(extra, res.at[0], sem.at[3]).wait()
    for copy in copies:
        copy.wait()


def moved_by(array, axis, by):
    n = lax.axis_size(axis)
    return lax.ppermute(array, axis, [(i, (i + by) % n) for i in range(n)])


def moved_down(array):
    count = lax.axis_size(ALL)
    return lax.ppermute(array, ALL, [(i, i - 1) for i in range(1, count)])


def on_device(weights, biases, states, guess, output_grad, coarse_rate):
    layers, width, _ = weights.shape
    batch = states.shape[1]
    half = width // 2
    parts = width // COLS
    plane = lax.axis_size(PLANE)
    dma = pltpu.SemaphoreType.DMA
    square = jax.ShapeDtypeStruct((batch, width), F32)

    weights, biases, states = in_hbm(weights), in_hbm(biases), in_hbm(states)
    guess, output_grad = in_hbm(guess), in_hbm(output_grad)
    moved, slopes, wv = pl.pallas_call(
        first_kernel,
        out_shape=(
            square,
            pltpu.VMEM((layers, batch, width), F32),
            pltpu.VMEM(weights.shape, BF16),
        ),
        in_specs=[HBM] * 4,
        out_specs=(VMEM,) * 3,
        scratch_shapes=[
            pltpu.VMEM(states.shape, BF16),
            pltpu.VMEM((batch, width), F32),
            pltpu.VMEM(biases.shape, F32),
            pltpu.VMEM(states.shape, BF16),
            dma((layers, parts)),
            dma((layers + 2,)),
        ],
        compiler_params=params(10),
        name="first",
    )(weights, biases, states, guess)
    slopes, wv = in_vmem(slopes), in_vmem(wv)

    above = moved_down(moved)
    rup = moved_by(coarse_rate, ALL, 1)

    first, res, keep, send, rest = pl.pallas_call(
        second_kernel,
        out_shape=(
            pltpu.HBM((batch, width), F32),
            square,
            jax.ShapeDtypeStruct((batch, half), F32),
            jax.ShapeDtypeStruct((batch + 8, half), F32),
            jax.ShapeDtypeStruct((batch, half), F32),
        ),
        in_specs=[HBM] * 2 + [VMEM] * 5,
        out_specs=(HBM,) + (VMEM,) * 4,
        scratch_shapes=[pltpu.VMEM((batch, width), F32)] * 2 + [dma((2,))],
        compiler_params=params(8),
        name="second",
    )(guess, output_grad, above, rup, moved, slopes, wv)

    got = moved_by(send, "c", 1)
    pieces = pl.pallas_call(
        chip_kernel,
        out_shape=jax.ShapeDtypeStruct((plane * PIECE, LANES), F32),
        in_specs=[VMEM] * 4,
        out_specs=VMEM,
        compiler_params=params(4),
        name="chip",
    )(keep, got, coarse_rate, rup)
    pieces = pieces.reshape(plane, PIECE, 1, LANES)
    maps = lax.all_to_all(pieces, PLANE, 0, 0).reshape(plane * PIECE, LANES)
    whole = pl.pallas_call(
        plane_kernel,
        out_shape=jax.ShapeDtypeStruct((ROWS + 8, LANES), F32),
        in_specs=[VMEM],
        out_specs=VMEM,
        compiler_params=params(4),
        name="plane",
    )(maps)
    higher = [moved_by(whole, "x", -k) for k in (1, 2, 3)]
    got_rest = moved_by(rest, "c", 1)
    got_res = moved_down(res)
    entering = pl.pallas_call(
        scan_kernel,
        out_shape=jax.ShapeDtypeStruct((plane, ROWS, LANES), F32),
        in_specs=[VMEM] * 4 + [HBM] * 2,
        out_specs=VMEM,
        compiler_params=params(4),
        name="scan",
    )(maps, *higher, got_res, got_rest)
    q_own = lax.all_to_all(entering, PLANE, 0, 0)
    q_other = moved_by(q_own, "c", 1)
    first, wv, sv = pl.pallas_call(
        fetch_kernel,
        out_shape=(
            pltpu.VMEM((batch, width), F32),
            pltpu.VMEM((layers - 1, width, width), BF16),
            pltpu.VMEM(states.shape, BF16),
        ),
        in_specs=[HBM] * 4,
        out_specs=(VMEM,) * 3,
        scratch_shapes=[dma((3,))],
        compiler_params=params(4),
        cost_estimate=pl.CostEstimate(flops=0, bytes_accessed=6 * MIB, transcendentals=0),
        name="fetch",
    )(in_hbm(first), weights, states, q_own)

    return pl.pallas_call(
        final_kernel,
        out_shape=(
            jax.ShapeDtypeStruct((1, batch, width), F32),
            jax.ShapeDtypeStruct(weights.shape, BF16),
            jax.ShapeDtypeStruct((1, batch, width), F32),
        ),
        in_specs=[VMEM] * 9 + [HBM] * 2,
        out_specs=(HBM,) * 3,
        scratch_shapes=[
            pltpu.VMEM((batch, width), F32),
            pltpu.VMEM((batch, width), F32),
            pltpu.VMEM((batch, width), F32),
            pltpu.VMEM(weights.shape, BF16),
            dma((4,)),
            dma((layers, width // PART)),
        ],
        compiler_params=params(16),
        name="final",
    )(
        q_own, q_other, got, got_rest, coarse_rate, slopes,
        in_vmem(first), in_vmem(wv), in_vmem(sv), output_grad, got_res,
    )


def solution(mesh):
    devices = mesh.devices
    grid = Mesh(devices.reshape(devices.shape[0], 4, -1, 2), ALL)
    blocks = P(ALL, None, None)
    return jax.shard_map(
        on_device,
        mesh=grid,
        in_specs=(blocks, P(ALL, None), blocks, blocks, P(), P(ALL, None)),
        out_specs=(blocks, blocks, blocks),
        check_vma=False,
    )
```

time: 616 us -> 76.5 us (0.12)
  waiting for transfers between devices: 286 us -> 16.4 us
  blocking collectives: 190 us -> 16.2 us
  other arithmetic: 87.9 us -> 0 us
  starting transfers between devices: 7.19 us -> 31 us
  matrix products: 15.2 us -> 0 us
  between operations: 14 us -> 0.73 us
  Pallas kernels: 0 us -> 11.9 us
  local copies, waits for them, and re-layouts: 8.06 us -> 0.01 us
    psum x1 -> x0, waiting for transfers between devices: 174 us -> none  [broadcast(): return lax.psum(block, axis)]
    psum x1 -> x0, blocking collectives: 126 us -> none  [broadcast(): return lax.psum(block, axis)]
    all_gather x2 -> x0, waiting for transfers between devices: 96.9 us -> none  [prefix(): gathered = jax.tree.map(lambda a: lax.all_gather(a, axis), part)]
    add x66 -> x0, other arithmetic: 82.6 us -> none  [the longest x65 81.6 us: compose(): later[0] * preceding_step[1] + later[1]]
    all_gather x2 -> x0, blocking collectives: 64.3 us -> none  [prefix(): gathered = jax.tree.map(lambda a: lax.all_gather(a, axis), part)]
    all_to_all x0 -> x1, blocking collectives: none -> 16.2 us  [on_device(): q_own = lax.all_to_all(entering, PLANE, 0, 0)]
    dot_general x8 -> x0, matrix products: 15.2 us -> none  [the longest x2 5.48 us: sweep(): jnp.einsum('bi,bj->ij', states[k], q, preferred_element_type=jnp.float32)]
    ppermute x2 -> x9, starting transfers between devices: 7.07 us -> 20.8 us  [the longest x7 13.3 us: moved_by(): return lax.ppermute(array, axis, [(i, (i + by) % n) for i in range(n)])]
  transfers between devices with their start and end apart: 5 -> 10, of which waited for: 4 -> 6; matrix products, arithmetic and copies ran while one was open for 0% -> 0% of each run, Pallas kernels for 0% -> 3%
where the time goes in v1:
time: 76.5 us; the launch traced here: 76.2 us
  starting transfers between devices  31 us (41%)
  waiting for transfers between devices  16.4 us (21%)
  blocking collectives  16.2 us (21%)
  Pallas kernels  11.9 us (16%)
    all_to_all x1, blocking collectives, on_device(): q_own = lax.all_to_all(entering, PLANE, 0, 0)  16.2 us
    ppermute x7, starting transfers between devices, moved_by(): return lax.ppermute(array, axis, [(i, (i + by) % n) for i in range(n)])  13.3 us
    all_to_all x1, starting transfers between devices, on_device(): maps = lax.all_to_all(pieces, PLANE, 0, 0).reshape(plane * PIECE, LANES)  10.2 us
    all_to_all x1, waiting for transfers between devices, on_device(): maps = lax.all_to_all(pieces, PLANE, 0, 0).reshape(plane * PIECE, LANES)  7.83 us
    ppermute x2, starting transfers between devices, moved_down(): return lax.ppermute(array, ALL, [(i, i - 1) for i in range(1, count)])  7.51 us
    ppermute x2, waiting for transfers between devices, moved_down(): return lax.ppermute(array, ALL, [(i, i - 1) for i in range(1, count)])  5.37 us
    pallas_call x1, Pallas kernels, on_device(): pl.pallas_call(first_kernel, out_shape=(square, pltpu.VMEM((layers, batch...  4.25 us
    ppermute x7, waiting for transfers between devices, moved_by(): return lax.ppermute(array, axis, [(i, (i + by) % n) for i in range(n)])  3.16 us
  transfers between devices with their start and end apart: 10, of which 6 were waited for; matrix products, arithmetic and copies ran while one was open for 0% of the time, Pallas kernels for 3%

profile of v1, /device:TPU:1, one launch (start us, length us, event | category | flops | bytes accessed | tf_op | source)
XLA Modules:
  0.0 76.2 jit_solution(14213988472208570361)
XLA Ops:
  0.6 0.0 copy-start
  0.6 4.2 %first.1 = (f32[128,1024]{1,0:T(8,128)S(1)}, f32[2,128,1024]{2,1,0:T(8,128)S(1)}, bf16[2,1024,1024]{2,1,0:T(8,128)(2,1)S(1)}) custom-call(bf16[2,1024,1024]{2,1,0:T(8,128)(2,1)} %w.3, f32[2,1024]{1,0:T(2,128)} %b.1, bf16[2,128,1024]{2,1,0:T(8,128)(2,1)} %s.3, f32[1,128,1024]{2,1,0:T(8,128)} %g.3), custom_call_target="tpu_custom_call" | custom-call | tf_op jit(solution)/shard_map/first/pallas_call | solution.py:279
  4.9 5.2 %collective-permute-start = (f32[128,1024]{1,0:T(8,128)S(1)}, f32[128,1024]{1,0:T(8,128)S(1)}, u32[]{:S(2)}, u32[]{:S(2)}) collective-permute-start(f32[128,1024]{1,0:T(8,128)S(1)} %get-tuple-element.14.moved), channel_id=1, source_target_pairs={{1,0},{2,1},{3,2},{4,3},{5,4},{6,5},{7,6},{8,7},{9,8},{10,9},{11,1... | collective-permute-start | bytes 1572872 | tf_op jit(solution)/shard_map/ppermute | solution.py:265
  10.1 0.0 copy-done
  10.1 0.1 collective-permute-start.1
  10.2 1.2 %collective-permute-done.1.rup = f32[1,1024]{1,0:T(1,128)S(1)} collective-permute-done((f32[1,1024]{1,0:T(1,128)S(1)}, f32[1,1024]{1,0:T(1,128)S(1)}, u32[]{:S(2)}, u32[]{:S(2)}) %collective-permute-start.1) | collective-permute-done | bytes 4128 | tf_op jit(solution)/shard_map/ppermute | solution.py:260
  11.3 5.4 %collective-permute-done.above = f32[128,1024]{1,0:T(8,128)S(1)} collective-permute-done((f32[128,1024]{1,0:T(8,128)S(1)}, f32[128,1024]{1,0:T(8,128)S(1)}, u32[]{:S(2)}, u32[]{:S(2)}) %collective-permute-start) | collective-permute-done | bytes 524320 | tf_op jit(solution)/shard_map/ppermute | solution.py:265
  16.7 1.7 %second.1 = (f32[128,1024]{1,0:T(8,128)}, f32[128,1024]{1,0:T(8,128)S(1)}, f32[128,512]{1,0:T(8,128)S(1)}, f32[136,512]{1,0:T(8,128)S(1)}, f32[128,512]{1,0:T(8,128)S(1)}) custom-call(f32[1,128,1024]{2,1,0:T(8,128)} %g.3, f32[128,1024]{1,0:T(8,128)} %og.3, f32[128,1024]{1,0:T(8,128)S(1)} %collective-permute-done.above, ...), custom_call_target="tpu_custom_call" | custom-call | tf_op jit(solution)/shard_map/second/pallas_call | solution.py:304
  18.4 3.7 %collective-permute-start.2 = (f32[136,512]{1,0:T(8,128)S(1)}, f32[136,512]{1,0:T(8,128)S(1)}, u32[]{:S(2)}, u32[]{:S(2)}) collective-permute-start(f32[136,512]{1,0:T(8,128)S(1)} %get-tuple-element.18), channel_id=1, source_target_pairs={{0,1},{1,0},{2,3},{3,2},{4,5},{5,4},{6,7},{7,6},{8,9},{9,8},{10,11... | collective-permute-start | bytes 835592 | tf_op jit(solution)/shard_map/ppermute | solution.py:260
  22.1 1.2 %collective-permute-done.2.got = f32[136,512]{1,0:T(8,128)S(1)} collective-permute-done((f32[136,512]{1,0:T(8,128)S(1)}, f32[136,512]{1,0:T(8,128)S(1)}, u32[]{:S(2)}, u32[]{:S(2)}) %collective-permute-start.2) | collective-permute-done | bytes 278560 | tf_op jit(solution)/shard_map/ppermute | solution.py:260
  23.3 0.8 chip.1
  24.1 10.2 %all-to-all-start = ((f32[32,17,1,128]{3,2,1,0:T(1,128)}), f32[32,17,1,128]{3,2,1,0:T(1,128)S(1)}, u32[]{:S(2)}, u32[]{:S(2)}) async-start(f32[32,17,1,128]{3,2,1,0:T(1,128)} %bitcast), calls=%async_computation | async-start | bytes 557056 | tf_op jit(solution)/shard_map/all_to_all | solution.py:330
  34.2 2.3 %collective-permute-start.6 = (f32[128,1024]{1,0:T(8,128)S(1)}, f32[128,1024]{1,0:T(8,128)S(1)}, u32[]{:S(2)}, u32[]{:S(2)}) collective-permute-start(f32[128,1024]{1,0:T(8,128)S(1)} %get-tuple-element.19), channel_id=1, source_target_pairs={{1,0},{2,1},{3,2},{4,3},{5,4},{6,5},{7,6},{8,7},{9,8},{10,9},{11,1... | collective-permute-start | bytes 1572872 | tf_op jit(solution)/shard_map/ppermute | solution.py:265
  36.6 0.1 collective-permute-start.7
  36.7 7.8 %all-to-all-done = f32[32,17,1,128]{3,2,1,0:T(1,128)S(1)} async-done(((f32[32,17,1,128]{3,2,1,0:T(1,128)}), f32[32,17,1,128]{3,2,1,0:T(1,128)S(1)}, u32[]{:S(2)}, u32[]{:S(2)}) %all-to-all-start) | async-done | bytes 278560 | tf_op jit(solution)/shard_map/all_to_all | solution.py:330
  44.5 0.1 plane.1
  44.6 1.3 %collective-permute-start.5 = (f32[24,128]{1,0:T(8,128)S(1)}, f32[24,128]{1,0:T(8,128)S(1)}, u32[]{:S(2)}, u32[]{:S(2)}) collective-permute-start(f32[24,128]{1,0:T(8,128)S(1)} %plane.1), channel_id=1, source_target_pairs={{0,64},{64,128},{128,192},{192,0},{1,65},{65,129},{129,193},{193,1... | collective-permute-start | bytes 36872 | tf_op jit(solution)/shard_map/ppermute | solution.py:260
  45.9 1.6 %collective-permute-start.4 = (f32[24,128]{1,0:T(8,128)S(1)}, f32[24,128]{1,0:T(8,128)S(1)}, u32[]{:S(2)}, u32[]{:S(2)}) collective-permute-start(f32[24,128]{1,0:T(8,128)S(1)} %plane.1), channel_id=1, source_target_pairs={{0,128},{64,192},{128,0},{192,64},{1,129},{65,193},{129,1},{193,65... | collective-permute-start | bytes 36872 | tf_op jit(solution)/shard_map/ppermute | solution.py:260
  47.5 2.0 %collective-permute-start.3 = (f32[24,128]{1,0:T(8,128)S(1)}, f32[24,128]{1,0:T(8,128)S(1)}, u32[]{:S(2)}, u32[]{:S(2)}) collective-permute-start(f32[24,128]{1,0:T(8,128)S(1)} %plane.1), channel_id=1, source_target_pairs={{0,192},{64,0},{128,64},{192,128},{1,193},{65,1},{129,65},{193,129... | collective-permute-start | bytes 36872 | tf_op jit(solution)/shard_map/ppermute | solution.py:260
  49.5 0.0 collective-permute-done.7.rest
  49.5 0.0 collective-permute-done.6.res.res_in
  49.5 0.0 collective-permute-done.5.three
  49.5 0.4 collective-permute-done.4.two
  49.9 0.4 collective-permute-done.3.one
  50.3 0.1 scan.1
  50.4 16.2 %all_to_all.10.after.q_own = f32[32,16,128]{2,1,0:T(8,128)S(1)} all-to-all(f32[32,16,128]{2,1,0:T(8,128)S(1)} %scan.1), channel_id=1, replica_groups=mesh['x'=4,'y'=4,'z'=8,'c'=2] {'y','z'}, dimensions={0} | all-to-all | bytes 524288 | tf_op jit(solution)/shard_map/all_to_all | solution.py:350
  66.6 4.5 %collective-permute-start.8 = (f32[32,16,128]{2,1,0:T(8,128)S(1)}, f32[32,16,128]{2,1,0:T(8,128)S(1)}, u32[]{:S(2)}, u32[]{:S(2)}) collective-permute-start(f32[32,16,128]{2,1,0:T(8,128)S(1)} %all_to_all.10.after.q_own), channel_id=1, source_target_pairs={{0,1},{1,0},{2,3},{3,2},{4,5},{5,4},{6,7},{7,6},{8,9},{9,8},{10,11... | collective-permute-start | bytes 786440 | tf_op jit(solution)/shard_map/ppermute | solution.py:260
  71.1 1.9 %fetch.1 = (f32[128,1024]{1,0:T(8,128)S(1)}, bf16[1,1024,1024]{2,1,0:T(8,128)(2,1)S(1)}, bf16[2,128,1024]{2,1,0:T(8,128)(2,1)S(1)}) custom-call(f32[128,1024]{1,0:T(8,128)} %get-tuple-element.21.first, bf16[2,1024,1024]{2,1,0:T(8,128)(2,1)} %w.3, bf16[2,128,1024]{2,1,0:T(8,128)(2,1)} %s.3, f32[32,16,128]{2,1,0:T(8,128)S(1)} %all_to_all.10.after.q_own), custom_call_target="tpu_custom_call" | custom-call | bytes 6291456 | tf_op jit(solution)/shard_map/fetch/pallas_call | solution.py:352
  73.1 0.0 collective-permute-done.8.q_other
  73.1 3.1 %final.1 = (f32[1,128,1024]{2,1,0:T(8,128)}, bf16[2,1024,1024]{2,1,0:T(8,128)(2,1)}, f32[1,128,1024]{2,1,0:T(8,128)}) custom-call(f32[32,16,128]{2,1,0:T(8,128)S(1)} %all_to_all.10.after.q_own, f32[32,16,128]{2,1,0:T(8,128)S(1)} %collective-permute-done.8.q_other, f32[136,512]{1,0:T(8,128)S(1)} %collective-permute-done.2.got, ...), custom_call_target="tpu_custom_call" | custom-call | tf_op jit(solution)/shard_map/final/pallas_call | solution.py:367
Async XLA Ops:
  0.6 9.4 %copy-start = (f32[1,1024]{1,0:T(1,128)S(1)}, f32[1,1024]{1,0:T(1,128)}, u32[]{:S(2)}) copy-start(f32[1,1024]{1,0:T(1,128)} %rate.3) | copy-start | bytes 12292
  4.9 11.8 %collective-permute-start = (f32[128,1024]{1,0:T(8,128)S(1)}, f32[128,1024]{1,0:T(8,128)S(1)}, u32[]{:S(2)}, u32[]{:S(2)}) collective-permute-start(f32[128,1024]{1,0:T(8,128)S(1)} %get-tuple-element.14.moved), channel_id=1, source_target_pairs={{1,0},{2,1},{3,2},{4,3},{5,4},{6,5},{7,6},{8,7},{9,8},{10,9},{11,1... | collective-permute-start | bytes 1572872 | tf_op jit(solution)/shard_map/ppermute | solution.py:265
  10.1 1.2 %collective-permute-start.1 = (f32[1,1024]{1,0:T(1,128)S(1)}, f32[1,1024]{1,0:T(1,128)S(1)}, u32[]{:S(2)}, u32[]{:S(2)}) collective-permute-start(f32[1,1024]{1,0:T(1,128)S(1)} %copy-done), channel_id=1, source_target_pairs={{0,1},{1,2},{2,3},{3,4},{4,5},{5,6},{6,7},{7,8},{8,9},{9,10},{10,1... | collective-permute-start | bytes 12296 | tf_op jit(solution)/shard_map/ppermute | solution.py:260
  18.4 4.9 %collective-permute-start.2 = (f32[136,512]{1,0:T(8,128)S(1)}, f32[136,512]{1,0:T(8,128)S(1)}, u32[]{:S(2)}, u32[]{:S(2)}) collective-permute-start(f32[136,512]{1,0:T(8,128)S(1)} %get-tuple-element.18), channel_id=1, source_target_pairs={{0,1},{1,0},{2,3},{3,2},{4,5},{5,4},{6,7},{7,6},{8,9},{9,8},{10,11... | collective-permute-start | bytes 835592 | tf_op jit(solution)/shard_map/ppermute | solution.py:260
  24.1 20.4 %all-to-all-start = ((f32[32,17,1,128]{3,2,1,0:T(1,128)}), f32[32,17,1,128]{3,2,1,0:T(1,128)S(1)}, u32[]{:S(2)}, u32[]{:S(2)}) async-start(f32[32,17,1,128]{3,2,1,0:T(1,128)} %bitcast), calls=%async_computation | async-start | bytes 557056 | tf_op jit(solution)/shard_map/all_to_all | solution.py:330
  34.2 15.3 %collective-permute-start.6 = (f32[128,1024]{1,0:T(8,128)S(1)}, f32[128,1024]{1,0:T(8,128)S(1)}, u32[]{:S(2)}, u32[]{:S(2)}) collective-permute-start(f32[128,1024]{1,0:T(8,128)S(1)} %get-tuple-element.19), channel_id=1, source_target_pairs={{1,0},{2,1},{3,2},{4,3},{5,4},{6,5},{7,6},{8,7},{9,8},{10,9},{11,1... | collective-permute-start | bytes 1572872 | tf_op jit(solution)/shard_map/ppermute | solution.py:265
  36.6 12.9 %collective-permute-start.7 = (f32[128,512]{1,0:T(8,128)S(1)}, f32[128,512]{1,0:T(8,128)S(1)}, u32[]{:S(2)}, u32[]{:S(2)}) collective-permute-start(f32[128,512]{1,0:T(8,128)S(1)} %get-tuple-element.20), channel_id=1, source_target_pairs={{0,1},{1,0},{2,3},{3,2},{4,5},{5,4},{6,7},{7,6},{8,9},{9,8},{10,11... | collective-permute-start | bytes 786440 | tf_op jit(solution)/shard_map/ppermute | solution.py:260
  44.6 4.9 %collective-permute-start.5 = (f32[24,128]{1,0:T(8,128)S(1)}, f32[24,128]{1,0:T(8,128)S(1)}, u32[]{:S(2)}, u32[]{:S(2)}) collective-permute-start(f32[24,128]{1,0:T(8,128)S(1)} %plane.1), channel_id=1, source_target_pairs={{0,64},{64,128},{128,192},{192,0},{1,65},{65,129},{129,193},{193,1... | collective-permute-start | bytes 36872 | tf_op jit(solution)/shard_map/ppermute | solution.py:260
  45.9 4.0 %collective-permute-start.4 = (f32[24,128]{1,0:T(8,128)S(1)}, f32[24,128]{1,0:T(8,128)S(1)}, u32[]{:S(2)}, u32[]{:S(2)}) collective-permute-start(f32[24,128]{1,0:T(8,128)S(1)} %plane.1), channel_id=1, source_target_pairs={{0,128},{64,192},{128,0},{192,64},{1,129},{65,193},{129,1},{193,65... | collective-permute-start | bytes 36872 | tf_op jit(solution)/shard_map/ppermute | solution.py:260
  47.5 2.8 %collective-permute-start.3 = (f32[24,128]{1,0:T(8,128)S(1)}, f32[24,128]{1,0:T(8,128)S(1)}, u32[]{:S(2)}, u32[]{:S(2)}) collective-permute-start(f32[24,128]{1,0:T(8,128)S(1)} %plane.1), channel_id=1, source_target_pairs={{0,192},{64,0},{128,64},{192,128},{1,193},{65,1},{129,65},{193,129... | collective-permute-start | bytes 36872 | tf_op jit(solution)/shard_map/ppermute | solution.py:260
  66.6 6.5 %collective-permute-start.8 = (f32[32,16,128]{2,1,0:T(8,128)S(1)}, f32[32,16,128]{2,1,0:T(8,128)S(1)}, u32[]{:S(2)}, u32[]{:S(2)}) collective-permute-start(f32[32,16,128]{2,1,0:T(8,128)S(1)} %all_to_all.10.after.q_own), channel_id=1, source_target_pairs={{0,1},{1,0},{2,3},{3,2},{4,5},{5,4},{6,7},{7,6},{8,9},{9,8},{10,11... | collective-permute-start | bytes 786440 | tf_op jit(solution)/shard_map/ppermute | solution.py:260

commit v2 on v1

--- a/solution.py
+++ b/solution.py
@@ -155,29 +155,31 @@
     return got[PIECE * j : PIECE * j + ROWS, :], got[PIECE * j + ROWS : PIECE * j + PIECE, :]
 
 
-def plane_kernel(got, out):
-    count = got.shape[0] // PIECE
+def plane_kernel(got, out, terms, factors):
+    count = terms.shape[0]
     t, f = piece(got, count - 1)
-    for j in reversed(range(count - 1)):
-        tj, fj = piece(got, j)
-        t = tj + fj * t
-        f = fj * f
+    for j in reversed(range(count)):
+        if j < count - 1:
+            tj, fj = piece(got, j)
+            t = tj + fj * t
+            f = fj * f
+        terms[j, :, :] = t
+        factors[j, :, :] = f
     out[:ROWS, :] = t
     out[ROWS:, :] = jnp.broadcast_to(f, (8, LANES))
 
 
-def scan_kernel(got, one, two, three, res, rest, out):
-    del res, rest
+def scan_kernel(terms, factors, one, two, three, res, rest, first, wv, sv, out):
+    del res, rest, first, wv, sv
     place, size = lax.axis_index("x"), lax.axis_size("x")
+    count = out.shape[0]
     carry = jnp.zeros((ROWS, LANES), F32)
     for k, b in ((3, three), (2, two), (1, one)):
         t, f = b[:ROWS, :], b[ROWS : ROWS + 1, :]
         carry = jnp.where(place + k < size, t + f * carry, carry)
-    for j in reversed(range(out.shape[0])):
-        out[j, :, :] = carry
-        if j:
-            t, f = piece(got, j)
-            carry = t + f * carry
+    out[count - 1, :, :] = carry
+    for j in range(count - 1):
+        out[j, :, :] = terms[j + 1] + factors[j + 1] * carry
 
 
 def fetch_kernel(first, w, s, after, first_v, wv, sv, sem):
@@ -328,27 +330,21 @@
     )(keep, got, coarse_rate, rup)
     pieces = pieces.reshape(plane, PIECE, 1, LANES)
     maps = lax.all_to_all(pieces, PLANE, 0, 0).reshape(plane * PIECE, LANES)
-    whole = pl.pallas_call(
+    whole, terms, factors = pl.pallas_call(
         plane_kernel,
-        out_shape=jax.ShapeDtypeStruct((ROWS + 8, LANES), F32),
+        out_shape=(
+            jax.ShapeDtypeStruct((ROWS + 8, LANES), F32),
+            jax.ShapeDtypeStruct((plane, ROWS, LANES), F32),
+            jax.ShapeDtypeStruct((plane, 1, LANES), F32),
+        ),
         in_specs=[VMEM],
-        out_specs=VMEM,
+        out_specs=(VMEM,) * 3,
         compiler_params=params(4),
         name="plane",
     )(maps)
     higher = [moved_by(whole, "x", -k) for k in (1, 2, 3)]
     got_rest = moved_by(rest, "c", 1)
     got_res = moved_down(res)
-    entering = pl.pallas_call(
-        scan_kernel,
-        out_shape=jax.ShapeDtypeStruct((plane, ROWS, LANES), F32),
-        in_specs=[VMEM] * 4 + [HBM] * 2,
-        out_specs=VMEM,
-        compiler_params=params(4),
-        name="scan",
-    )(maps, *higher, got_res, got_rest)
-    q_own = lax.all_to_all(entering, PLANE, 0, 0)
-    q_other = moved_by(q_own, "c", 1)
     first, wv, sv = pl.pallas_call(
         fetch_kernel,
         out_shape=(
@@ -362,8 +358,18 @@
         compiler_params=params(4),
         cost_estimate=pl.CostEstimate(flops=0, bytes_accessed=6 * MIB, transcendentals=0),
         name="fetch",
-    )(in_hbm(first), weights, states, q_own)
-
+    )(in_hbm(first), weights, states, whole)
+    first, wv, sv = in_vmem(first), in_vmem(wv), in_vmem(sv)
+    entering = pl.pallas_call(
+        scan_kernel,
+        out_shape=jax.ShapeDtypeStruct((plane, ROWS, LANES), F32),
+        in_specs=[VMEM] * 5 + [HBM] * 2 + [VMEM] * 3,
+        out_specs=VMEM,
+        compiler_params=params(4),
+        name="scan",
+    )(terms, factors, *higher, got_res, got_rest, first, wv, sv)
+    q_own = lax.all_to_all(entering, PLANE, 0, 0)
+    q_other = moved_by(q_own, "c", 1)
     return pl.pallas_call(
         final_kernel,
         out_shape=(
@@ -385,7 +391,7 @@
         name="final",
     )(
         q_own, q_other, got, got_rest, coarse_rate, slopes,
-        in_vmem(first), in_vmem(wv), in_vmem(sv), output_grad, got_res,
+        first, wv, sv, output_grad, got_res,
     )
 
 

time: 76.5 us -> 76 us (level)
  starting transfers between devices: 31 us -> 30.1 us
    ppermute x7, starting transfers between devices: 13.3 us -> 12.5 us  [moved_by(): return lax.ppermute(array, axis, [(i, (i + by) % n) for i in range(n)])]
  transfers between devices with their start and end apart: 10 -> 10, of which waited for: 6 -> 5; matrix products, arithmetic and copies ran while one was open for 0% -> 0% of each run, Pallas kernels for 3% -> 3%
where the time goes in v2:
time: 76 us; the launch traced here: 75.7 us
  starting transfers between devices  30.1 us (40%)
  waiting for transfers between devices  16.7 us (22%)
  blocking collectives  16.2 us (21%)
  Pallas kernels  11.9 us (16%)
  between operations  0.76 us (1%)
    all_to_all x1, blocking collectives, on_device(): q_own = lax.all_to_all(entering, PLANE, 0, 0)  16.2 us
    ppermute x7, starting transfers between devices, moved_by(): return lax.ppermute(array, axis, [(i, (i + by) % n) for i in range(n)])  12.5 us
    all_to_all x1, starting transfers between devices, on_device(): maps = lax.all_to_all(pieces, PLANE, 0, 0).reshape(plane * PIECE, LANES)  10.2 us
    all_to_all x1, waiting for transfers between devices, on_device(): maps = lax.all_to_all(pieces, PLANE, 0, 0).reshape(plane * PIECE, LANES)  7.83 us
    ppermute x2, starting transfers between devices, moved_down(): return lax.ppermute(array, ALL, [(i, i - 1) for i in range(1, count)])  7.51 us
    ppermute x2, waiting for transfers between devices, moved_down(): return lax.ppermute(array, ALL, [(i, i - 1) for i in range(1, count)])  5.37 us
    pallas_call x1, Pallas kernels, on_device(): pl.pallas_call(first_kernel, out_shape=(square, pltpu.VMEM((layers, batch...  4.25 us
    ppermute x7, waiting for transfers between devices, moved_by(): return lax.ppermute(array, axis, [(i, (i + by) % n) for i in range(n)])  3.51 us
  transfers between devices with their start and end apart: 10, of which 5 were waited for; matrix products, arithmetic and copies ran while one was open for 0% of the time, Pallas kernels for 3%

profile of v2, /device:TPU:1, one launch (start us, length us, event | category | flops | bytes accessed | tf_op | source)
XLA Modules:
  0.0 75.7 jit_solution(654724178480534526)
XLA Ops:
  0.6 0.0 copy-start
  0.6 4.2 %first.1 = (f32[128,1024]{1,0:T(8,128)S(1)}, f32[2,128,1024]{2,1,0:T(8,128)S(1)}, bf16[2,1024,1024]{2,1,0:T(8,128)(2,1)S(1)}) custom-call(bf16[2,1024,1024]{2,1,0:T(8,128)(2,1)} %w.3, f32[2,1024]{1,0:T(2,128)} %b.1, bf16[2,128,1024]{2,1,0:T(8,128)(2,1)} %s.3, f32[1,128,1024]{2,1,0:T(8,128)} %g.3), custom_call_target="tpu_custom_call" | custom-call | tf_op jit(solution)/shard_map/first/pallas_call | solution.py:281
  4.9 5.2 %collective-permute-start = (f32[128,1024]{1,0:T(8,128)S(1)}, f32[128,1024]{1,0:T(8,128)S(1)}, u32[]{:S(2)}, u32[]{:S(2)}) collective-permute-start(f32[128,1024]{1,0:T(8,128)S(1)} %get-tuple-element.17.moved), channel_id=1, source_target_pairs={{1,0},{2,1},{3,2},{4,3},{5,4},{6,5},{7,6},{8,7},{9,8},{10,9},{11,1... | collective-permute-start | bytes 1572872 | tf_op jit(solution)/shard_map/ppermute | solution.py:267
  10.1 0.0 copy-done
  10.1 0.1 collective-permute-start.1
  10.2 1.2 %collective-permute-done.1.rup = f32[1,1024]{1,0:T(1,128)S(1)} collective-permute-done((f32[1,1024]{1,0:T(1,128)S(1)}, f32[1,1024]{1,0:T(1,128)S(1)}, u32[]{:S(2)}, u32[]{:S(2)}) %collective-permute-start.1) | collective-permute-done | bytes 4128 | tf_op jit(solution)/shard_map/ppermute | solution.py:262
  11.3 5.4 %collective-permute-done.above = f32[128,1024]{1,0:T(8,128)S(1)} collective-permute-done((f32[128,1024]{1,0:T(8,128)S(1)}, f32[128,1024]{1,0:T(8,128)S(1)}, u32[]{:S(2)}, u32[]{:S(2)}) %collective-permute-start) | collective-permute-done | bytes 524320 | tf_op jit(solution)/shard_map/ppermute | solution.py:267
  16.7 1.7 %second.1 = (f32[128,1024]{1,0:T(8,128)}, f32[128,1024]{1,0:T(8,128)S(1)}, f32[128,512]{1,0:T(8,128)S(1)}, f32[136,512]{1,0:T(8,128)S(1)}, f32[128,512]{1,0:T(8,128)S(1)}) custom-call(f32[1,128,1024]{2,1,0:T(8,128)} %g.3, f32[128,1024]{1,0:T(8,128)} %og.3, f32[128,1024]{1,0:T(8,128)S(1)} %collective-permute-done.above, ...), custom_call_target="tpu_custom_call" | custom-call | tf_op jit(solution)/shard_map/second/pallas_call | solution.py:306
  18.4 3.7 %collective-permute-start.2 = (f32[136,512]{1,0:T(8,128)S(1)}, f32[136,512]{1,0:T(8,128)S(1)}, u32[]{:S(2)}, u32[]{:S(2)}) collective-permute-start(f32[136,512]{1,0:T(8,128)S(1)} %get-tuple-element.21), channel_id=1, source_target_pairs={{0,1},{1,0},{2,3},{3,2},{4,5},{5,4},{6,7},{7,6},{8,9},{9,8},{10,11... | collective-permute-start | bytes 835592 | tf_op jit(solution)/shard_map/ppermute | solution.py:262
  22.1 1.2 %collective-permute-done.2.got = f32[136,512]{1,0:T(8,128)S(1)} collective-permute-done((f32[136,512]{1,0:T(8,128)S(1)}, f32[136,512]{1,0:T(8,128)S(1)}, u32[]{:S(2)}, u32[]{:S(2)}) %collective-permute-start.2) | collective-permute-done | bytes 278560 | tf_op jit(solution)/shard_map/ppermute | solution.py:262
  23.3 0.8 %chip.1 = f32[544,128]{1,0:T(8,128)} custom-call(f32[128,512]{1,0:T(8,128)S(1)} %get-tuple-element.20.keep, f32[136,512]{1,0:T(8,128)S(1)} %collective-permute-done.2.got, f32[1,1024]{1,0:T(1,128)S(1)} %copy-done, f32[1,1024]{1,0:T(1,128)S(1)} %collective-permute-done.1.rup), custom_call_target="tpu_custom_call" | custom-call | tf_op jit(solution)/shard_map/chip/pallas_call | solution.py:323
  24.1 10.2 %all-to-all-start = ((f32[32,17,1,128]{3,2,1,0:T(1,128)}), f32[32,17,1,128]{3,2,1,0:T(1,128)S(1)}, u32[]{:S(2)}, u32[]{:S(2)}) async-start(f32[32,17,1,128]{3,2,1,0:T(1,128)} %bitcast), calls=%async_computation | async-start | bytes 557056 | tf_op jit(solution)/shard_map/all_to_all | solution.py:332
  34.2 2.3 %collective-permute-start.6 = (f32[128,1024]{1,0:T(8,128)S(1)}, f32[128,1024]{1,0:T(8,128)S(1)}, u32[]{:S(2)}, u32[]{:S(2)}) collective-permute-start(f32[128,1024]{1,0:T(8,128)S(1)} %get-tuple-element.25), channel_id=1, source_target_pairs={{1,0},{2,1},{3,2},{4,3},{5,4},{6,5},{7,6},{8,7},{9,8},{10,9},{11,1... | collective-permute-start | bytes 1572872 | tf_op jit(solution)/shard_map/ppermute | solution.py:267
  36.6 0.1 collective-permute-start.7
  36.7 7.8 %all-to-all-done = f32[32,17,1,128]{3,2,1,0:T(1,128)S(1)} async-done(((f32[32,17,1,128]{3,2,1,0:T(1,128)}), f32[32,17,1,128]{3,2,1,0:T(1,128)S(1)}, u32[]{:S(2)}, u32[]{:S(2)}) %all-to-all-start) | async-done | bytes 278560 | tf_op jit(solution)/shard_map/all_to_all | solution.py:332
  44.5 0.1 plane.1
  44.6 1.3 %collective-permute-start.5 = (f32[24,128]{1,0:T(8,128)S(1)}, f32[24,128]{1,0:T(8,128)S(1)}, u32[]{:S(2)}, u32[]{:S(2)}) collective-permute-start(f32[24,128]{1,0:T(8,128)S(1)} %get-tuple-element.24.after), channel_id=1, source_target_pairs={{0,64},{64,128},{128,192},{192,0},{1,65},{65,129},{129,193},{193,1... | collective-permute-start | bytes 36872 | tf_op jit(solution)/shard_map/ppermute | solution.py:262
  45.9 1.6 %collective-permute-start.4 = (f32[24,128]{1,0:T(8,128)S(1)}, f32[24,128]{1,0:T(8,128)S(1)}, u32[]{:S(2)}, u32[]{:S(2)}) collective-permute-start(f32[24,128]{1,0:T(8,128)S(1)} %get-tuple-element.24.after), channel_id=1, source_target_pairs={{0,128},{64,192},{128,0},{192,64},{1,129},{65,193},{129,1},{193,65... | collective-permute-start | bytes 36872 | tf_op jit(solution)/shard_map/ppermute | solution.py:262
  47.5 2.0 %collective-permute-start.3 = (f32[24,128]{1,0:T(8,128)S(1)}, f32[24,128]{1,0:T(8,128)S(1)}, u32[]{:S(2)}, u32[]{:S(2)}) collective-permute-start(f32[24,128]{1,0:T(8,128)S(1)} %get-tuple-element.24.after), channel_id=1, source_target_pairs={{0,192},{64,0},{128,64},{192,128},{1,193},{65,1},{129,65},{193,129... | collective-permute-start | bytes 36872 | tf_op jit(solution)/shard_map/ppermute | solution.py:262
  49.5 1.9 %fetch.1 = (f32[128,1024]{1,0:T(8,128)S(1)}, bf16[1,1024,1024]{2,1,0:T(8,128)(2,1)S(1)}, bf16[2,128,1024]{2,1,0:T(8,128)(2,1)S(1)}) custom-call(f32[128,1024]{1,0:T(8,128)} %get-tuple-element.27.first, bf16[2,1024,1024]{2,1,0:T(8,128)(2,1)} %w.3, bf16[2,128,1024]{2,1,0:T(8,128)(2,1)} %s.3, f32[24,128]{1,0:T(8,128)S(1)} %get-tuple-element.24.after), custom_call_target="tpu_custom_call" | custom-call | bytes 6291456 | tf_op jit(solution)/shard_map/fetch/pallas_call | solution.py:348
  51.4 0.0 collective-permute-done.7.rest
  51.5 0.0 collective-permute-done.6.res.res_in
  51.5 0.0 collective-permute-done.5.three
  51.5 0.0 collective-permute-done.4.two
  51.5 0.0 collective-permute-done.3.one
  51.5 16.2 %all_to_all.10.q_own = f32[32,16,128]{2,1,0:T(8,128)S(1)} all-to-all(f32[32,16,128]{2,1,0:T(8,128)S(1)} %scan.1), channel_id=1, replica_groups=mesh['x'=4,'y'=4,'z'=8,'c'=2] {'y','z'}, dimensions={0} | all-to-all | bytes 524288 | tf_op jit(solution)/shard_map/all_to_all | solution.py:371
  67.7 3.7 %collective-permute-start.8 = (f32[32,16,128]{2,1,0:T(8,128)S(1)}, f32[32,16,128]{2,1,0:T(8,128)S(1)}, u32[]{:S(2)}, u32[]{:S(2)}) collective-permute-start(f32[32,16,128]{2,1,0:T(8,128)S(1)} %all_to_all.10.q_own), channel_id=1, source_target_pairs={{0,1},{1,0},{2,3},{3,2},{4,5},{5,4},{6,7},{7,6},{8,9},{9,8},{10,11... | collective-permute-start | bytes 786440 | tf_op jit(solution)/shard_map/ppermute | solution.py:262
  71.4 1.2 %collective-permute-done.8.q_other = f32[32,16,128]{2,1,0:T(8,128)S(1)} collective-permute-done((f32[32,16,128]{2,1,0:T(8,128)S(1)}, f32[32,16,128]{2,1,0:T(8,128)S(1)}, u32[]{:S(2)}, u32[]{:S(2)}) %collective-permute-start.8) | collective-permute-done | bytes 262176 | tf_op jit(solution)/shard_map/ppermute | solution.py:262
  72.6 3.1 %final.1 = (f32[1,128,1024]{2,1,0:T(8,128)}, bf16[2,1024,1024]{2,1,0:T(8,128)(2,1)}, f32[1,128,1024]{2,1,0:T(8,128)}) custom-call(f32[32,16,128]{2,1,0:T(8,128)S(1)} %all_to_all.10.q_own, f32[32,16,128]{2,1,0:T(8,128)S(1)} %collective-permute-done.8.q_other, f32[136,512]{1,0:T(8,128)S(1)} %collective-permute-done.2.got, ...), custom_call_target="tpu_custom_call" | custom-call | tf_op jit(solution)/shard_map/final/pallas_call | solution.py:373
  (1 shorter events, 0.0 us)
Async XLA Ops:
  0.6 9.4 %copy-start = (f32[1,1024]{1,0:T(1,128)S(1)}, f32[1,1024]{1,0:T(1,128)}, u32[]{:S(2)}) copy-start(f32[1,1024]{1,0:T(1,128)} %rate.3) | copy-start | bytes 12292
  4.9 11.8 %collective-permute-start = (f32[128,1024]{1,0:T(8,128)S(1)}, f32[128,1024]{1,0:T(8,128)S(1)}, u32[]{:S(2)}, u32[]{:S(2)}) collective-permute-start(f32[128,1024]{1,0:T(8,128)S(1)} %get-tuple-element.17.moved), channel_id=1, source_target_pairs={{1,0},{2,1},{3,2},{4,3},{5,4},{6,5},{7,6},{8,7},{9,8},{10,9},{11,1... | collective-permute-start | bytes 1572872 | tf_op jit(solution)/shard_map/ppermute | solution.py:267
  10.1 1.2 %collective-permute-start.1 = (f32[1,1024]{1,0:T(1,128)S(1)}, f32[1,1024]{1,0:T(1,128)S(1)}, u32[]{:S(2)}, u32[]{:S(2)}) collective-permute-start(f32[1,1024]{1,0:T(1,128)S(1)} %copy-done), channel_id=1, source_target_pairs={{0,1},{1,2},{2,3},{3,4},{4,5},{5,6},{6,7},{7,8},{8,9},{9,10},{10,1... | collective-permute-start | bytes 12296 | tf_op jit(solution)/shard_map/ppermute | solution.py:262
  18.4 4.9 %collective-permute-start.2 = (f32[136,512]{1,0:T(8,128)S(1)}, f32[136,512]{1,0:T(8,128)S(1)}, u32[]{:S(2)}, u32[]{:S(2)}) collective-permute-start(f32[136,512]{1,0:T(8,128)S(1)} %get-tuple-element.21), channel_id=1, source_target_pairs={{0,1},{1,0},{2,3},{3,2},{4,5},{5,4},{6,7},{7,6},{8,9},{9,8},{10,11... | collective-permute-start | bytes 835592 | tf_op jit(solution)/shard_map/ppermute | solution.py:262
  24.1 20.4 %all-to-all-start = ((f32[32,17,1,128]{3,2,1,0:T(1,128)}), f32[32,17,1,128]{3,2,1,0:T(1,128)S(1)}, u32[]{:S(2)}, u32[]{:S(2)}) async-start(f32[32,17,1,128]{3,2,1,0:T(1,128)} %bitcast), calls=%async_computation | async-start | bytes 557056 | tf_op jit(solution)/shard_map/all_to_all | solution.py:332
  34.2 17.2 %collective-permute-start.6 = (f32[128,1024]{1,0:T(8,128)S(1)}, f32[128,1024]{1,0:T(8,128)S(1)}, u32[]{:S(2)}, u32[]{:S(2)}) collective-permute-start(f32[128,1024]{1,0:T(8,128)S(1)} %get-tuple-element.25), channel_id=1, source_target_pairs={{1,0},{2,1},{3,2},{4,3},{5,4},{6,5},{7,6},{8,7},{9,8},{10,9},{11,1... | collective-permute-start | bytes 1572872 | tf_op jit(solution)/shard_map/ppermute | solution.py:267
  36.6 14.9 %collective-permute-start.7 = (f32[128,512]{1,0:T(8,128)S(1)}, f32[128,512]{1,0:T(8,128)S(1)}, u32[]{:S(2)}, u32[]{:S(2)}) collective-permute-start(f32[128,512]{1,0:T(8,128)S(1)} %get-tuple-element.26), channel_id=1, source_target_pairs={{0,1},{1,0},{2,3},{3,2},{4,5},{5,4},{6,7},{7,6},{8,9},{9,8},{10,11... | collective-permute-start | bytes 786440 | tf_op jit(solution)/shard_map/ppermute | solution.py:262
  44.6 6.9 %collective-permute-start.5 = (f32[24,128]{1,0:T(8,128)S(1)}, f32[24,128]{1,0:T(8,128)S(1)}, u32[]{:S(2)}, u32[]{:S(2)}) collective-permute-start(f32[24,128]{1,0:T(8,128)S(1)} %get-tuple-element.24.after), channel_id=1, source_target_pairs={{0,64},{64,128},{128,192},{192,0},{1,65},{65,129},{129,193},{193,1... | collective-permute-start | bytes 36872 | tf_op jit(solution)/shard_map/ppermute | solution.py:262
  45.9 5.6 %collective-permute-start.4 = (f32[24,128]{1,0:T(8,128)S(1)}, f32[24,128]{1,0:T(8,128)S(1)}, u32[]{:S(2)}, u32[]{:S(2)}) collective-permute-start(f32[24,128]{1,0:T(8,128)S(1)} %get-tuple-element.24.after), channel_id=1, source_target_pairs={{0,128},{64,192},{128,0},{192,64},{1,129},{65,193},{129,1},{193,65... | collective-permute-start | bytes 36872 | tf_op jit(solution)/shard_map/ppermute | solution.py:262
  47.5 4.0 %collective-permute-start.3 = (f32[24,128]{1,0:T(8,128)S(1)}, f32[24,128]{1,0:T(8,128)S(1)}, u32[]{:S(2)}, u32[]{:S(2)}) collective-permute-start(f32[24,128]{1,0:T(8,128)S(1)} %get-tuple-element.24.after), channel_id=1, source_target_pairs={{0,192},{64,0},{128,64},{192,128},{1,193},{65,1},{129,65},{193,129... | collective-permute-start | bytes 36872 | tf_op jit(solution)/shard_map/ppermute | solution.py:262
  67.7 4.8 %collective-permute-start.8 = (f32[32,16,128]{2,1,0:T(8,128)S(1)}, f32[32,16,128]{2,1,0:T(8,128)S(1)}, u32[]{:S(2)}, u32[]{:S(2)}) collective-permute-start(f32[32,16,128]{2,1,0:T(8,128)S(1)} %all_to_all.10.q_own), channel_id=1, source_target_pairs={{0,1},{1,0},{2,3},{3,2},{4,5},{5,4},{6,7},{7,6},{8,9},{9,8},{10,11... | collective-permute-start | bytes 786440 | tf_op jit(solution)/shard_map/ppermute | solution.py:262

commit v3 on v2

--- a/solution.py
+++ b/solution.py
@@ -10,6 +10,7 @@
 ALL = ("x", "y", "z", "c")
 PLANE = ("y", "z")
 MIB = 1024 * 1024
+HALF = 512
 F32 = jnp.float32
 BF16 = jnp.bfloat16
 HBM = pl.BlockSpec(memory_space=pl.ANY)
@@ -195,63 +196,126 @@
         copy.wait()
 
 
+def gathered(pieces):
+    blocks = HALF // LANES
+    rows = [
+        jnp.concatenate([pieces[r * blocks + n] for n in range(blocks)], axis=1)
+        for r in range(pieces.shape[0] // blocks)
+    ]
+    return jnp.concatenate(rows, axis=0)
+
+
+def top_extra(og, first, extra, sem):
+    top = is_top()
+
+    @pl.when(top)
+    def _():
+        one = pltpu.make_async_copy(og, extra, sem)
+        one.start()
+        one.wait()
+        extra[...] = extra[...] - first[...]
+
+    @pl.when(jnp.logical_not(top))
+    def _():
+        extra[...] = jnp.zeros_like(extra)
+
+
+def half_product(core0, out, q, wv, k):
+    top, half = wv.shape[0] - 1, q.shape[1]
+
+    @pl.when(core0 == (k == 0))
+    def _():
+        out[...] = times_transposed(q[...], wv[top, :, :half])
+
+    @pl.when(core0 != (k == 0))
+    def _():
+        out[...] = times_transposed(q[...], wv[top, :, half:])
+
+
+def own_kernel(q_own, got, rate, slopes, first, wv, sv, og, lam_h, g_h, part, q_h, extra, sem):
+    core0 = lax.axis_index("c") == 0
+    batch, half = lam_h.shape
+    l = slopes.shape[0] - 1
+    top_extra(og, first, extra, sem.at[0])
+    f = jnp.exp(-rate[...])
+    e = gathered(q_own)
+    err = jnp.where(core0, f[:, :half] * e + got[:batch, :], e + extra[:, half:])
+    lam = jnp.where(core0, first[:, :half], first[:, half:]) + err
+    lam_h[...] = lam
+    q = (lam * jnp.where(core0, slopes[l, :, :half], slopes[l, :, half:])).astype(BF16)
+    q_h[...] = q
+    half_product(core0, part, q_h, wv, 0)
+    for n in range(g_h.shape[0] // PART):
+        rows = slice(n * PART, (n + 1) * PART)
+        g_h[rows, :] = (transposed_times(sv[l, :, rows], q) * (0.5 / batch)).astype(BF16)
+
+
 def final_kernel(
-    q_own, q_other, got, rest, rate, slopes, first, wv, sv, og, res_in,
-    corrected, grads, res, lam_v, err_v, extra, gbuf, sem, gsem,
+    q_other, rest, rate, slopes, first, wv, sv, lam_h, g_h, part, og, res_in,
+    corrected, grads, res, lam_v, q_o, more, extra, gbuf, g_o, sem, gsem,
 ):
     top = is_top()
     core0 = lax.axis_index("c") == 0
     batch, width = lam_v.shape
     half = width // 2
-    blocks = half // LANES
     layers = slopes.shape[0]
+    l = layers - 1
+    low, high = pl.ds(0, half), pl.ds(half, half)
+
+    def columns(buf, k):
+        @pl.when(core0)
+        def _():
+            pltpu.make_async_copy(buf, grads.at[l, :, (low, high)[k]], sem.at[k]).start()
+
+        @pl.when(jnp.logical_not(core0))
+        def _():
+            pltpu.make_async_copy(buf, grads.at[l, :, (high, low)[k]], sem.at[k]).start()
+
+    columns(g_h, 0)
+    top_extra(og, first, extra, sem.at[3])
 
     @pl.when(top)
     def _():
-        one = pltpu.make_async_copy(og, extra, sem.at[3])
-        one.start()
-        one.wait()
-
-    @pl.when(top)
-    def _():
-        extra[...] = extra[...] - first[...]
         pltpu.make_async_copy(extra, res.at[0], sem.at[3]).start()
 
     @pl.when(jnp.logical_not(top))
     def _():
-        extra[...] = jnp.zeros_like(extra)
         pltpu.make_async_copy(res_in, res.at[0], sem.at[3]).start()
 
     f = jnp.exp(-rate[...])
-    for j in range(q_own.shape[0]):
-        r, n = j // blocks, j % blocks
-        rows = slice(r * ROWS, (r + 1) * ROWS)
-        for h in range(2):
-            cols = slice(h * half + n * LANES, h * half + (n + 1) * LANES)
-            e = jnp.where(core0 == (h == 0), q_own[j], q_other[j])
-            lower = (got, rest)[h][rows, n * LANES : (n + 1) * LANES]
-            err = jnp.where(core0, f[:, cols] * e + lower, e + extra[rows, cols])
-            err_v[rows, cols] = err
-
-    lam = first[...] + err_v[...]
-    lam_v[...] = lam
-    keep = pltpu.make_async_copy(lam_v, corrected.at[0], sem.at[0])
+    e = gathered(q_other)
+    err = jnp.where(core0, f[:, half:] * e + rest[...], e + extra[:, :half])
+    other = jnp.where(core0, first[:, half:], first[:, :half]) + err
+    q = (other * jnp.where(core0, slopes[l, :, half:], slopes[l, :, :half])).astype(BF16)
+    q_o[...] = q
+    half_product(core0, more, q_o, wv, 1)
+    for n in range(width // PART):
+        rows = slice(n * PART, (n + 1) * PART)
+        g_o[rows, :] = (transposed_times(sv[l, :, rows], q) * (0.5 / batch)).astype(BF16)
+    columns(g_o, 1)
+    own = lam_h[...]
+    lam_v[:, :half] = jnp.where(core0, own, other)
+    lam_v[:, half:] = jnp.where(core0, other, own)
+    keep = pltpu.make_async_copy(lam_v, corrected.at[0], sem.at[2])
     keep.start()
-    parts = width // PART
     copies = []
-    for l in reversed(range(layers)):
-        q = (lam * slopes[l]).astype(BF16)
-        for n in range(parts):
+    lam, product = lam_v[...], part[...] + more[...]
+    for k in reversed(range(l)):
+        lam = lam + 0.5 * product
+        q = (lam * slopes[k]).astype(BF16)
+        for n in range(width // PART):
             rows = slice(n * PART, (n + 1) * PART)
-            out = transposed_times(sv[l, :, rows], q) * (0.5 / batch)
-            gbuf[l, rows, :] = out.astype(BF16)
-            there = grads.at[l, pl.ds(n * PART, PART)]
-            copy = pltpu.make_async_copy(gbuf.at[l, pl.ds(n * PART, PART)], there, gsem.at[l, n])
+            out = transposed_times(sv[k, :, rows], q) * (0.5 / batch)
+            gbuf[k, rows, :] = out.astype(BF16)
+            there = grads.at[k, pl.ds(n * PART, PART)]
+            copy = pltpu.make_async_copy(gbuf.at[k, pl.ds(n * PART, PART)], there, gsem.at[k, n])
             copy.start()
             copies.append(copy)
-        if l:
-            lam = lam + 0.5 * times_transposed(q, wv[l - 1])
+        if k:
+            product = times_transposed(q, wv[k - 1])
     keep.wait()
+    pltpu.make_async_copy(g_h, grads.at[l, :, low], sem.at[0]).wait()
+    pltpu.make_async_copy(g_o, grads.at[l, :, low], sem.at[1]).wait()
     pltpu.make_async_copy(extra, res.at[0], sem.at[3]).wait()
     for copy in copies:
         copy.wait()
@@ -370,6 +434,20 @@
     )(terms, factors, *higher, got_res, got_rest, first, wv, sv)
     q_own = lax.all_to_all(entering, PLANE, 0, 0)
     q_other = moved_by(q_own, "c", 1)
+    lam_h, g_h, part = pl.pallas_call(
+        own_kernel,
+        out_shape=(
+            pltpu.VMEM((batch, half), F32),
+            pltpu.VMEM((width, half), BF16),
+            pltpu.VMEM((batch, width), F32),
+        ),
+        in_specs=[VMEM] * 7 + [HBM],
+        out_specs=(VMEM,) * 3,
+        scratch_shapes=[pltpu.VMEM((batch, half), BF16), pltpu.VMEM((batch, width), F32), dma((1,))],
+        compiler_params=params(8),
+        cost_estimate=pl.CostEstimate(flops=140000000, bytes_accessed=4 * MIB, transcendentals=0),
+        name="own",
+    )(q_own, got, coarse_rate, slopes, first, wv, sv, output_grad)
     return pl.pallas_call(
         final_kernel,
         out_shape=(
@@ -377,21 +455,23 @@
             jax.ShapeDtypeStruct(weights.shape, BF16),
             jax.ShapeDtypeStruct((1, batch, width), F32),
         ),
-        in_specs=[VMEM] * 9 + [HBM] * 2,
+        in_specs=[VMEM] * 10 + [HBM] * 2,
         out_specs=(HBM,) * 3,
         scratch_shapes=[
             pltpu.VMEM((batch, width), F32),
-            pltpu.VMEM((batch, width), F32),
-            pltpu.VMEM((batch, width), F32),
-            pltpu.VMEM(weights.shape, BF16),
+            pltpu.VMEM((batch, half), BF16),
+            pltpu.VMEM((batch, width), F32),
+            pltpu.VMEM((batch, width), F32),
+            pltpu.VMEM((layers - 1, width, width), BF16),
+            pltpu.VMEM((width, half), BF16),
             dma((4,)),
-            dma((layers, width // PART)),
+            dma((layers - 1, width // PART)),
         ],
-        compiler_params=params(16),
+        compiler_params=params(14),
         name="final",
     )(
-        q_own, q_other, got, got_rest, coarse_rate, slopes,
-        first, wv, sv, output_grad, got_res,
+        q_other, got_rest, coarse_rate, slopes, first, wv, sv,
+        in_vmem(lam_h), in_vmem(g_h), in_vmem(part), output_grad, got_res,
     )
 
 

time: 76 us -> 75.9 us (level)
  waiting for transfers between devices: 16.7 us -> 15.6 us
  Pallas kernels: 11.9 us -> 12.9 us
    ppermute x7, waiting for transfers between devices: 3.51 us -> 2.38 us  [moved_by(): return lax.ppermute(array, axis, [(i, (i + by) % n) for i in range(n)])]
    pallas_call x0 -> x1, Pallas kernels: none -> 1.12 us  [on_device(): pl.pallas_call(own_kernel, out_shape=(pltpu.VMEM((batch, half), F32), plt...]
  transfers between devices with their start and end apart: 10 -> 10, of which waited for: 5 -> 4; matrix products, arithmetic and copies ran while one was open for 0% -> 0% of each run, Pallas kernels for 3% -> 4%
where the time goes in v3:
time: 75.9 us; the launch traced here: 75.6 us
  starting transfers between devices  30.1 us (40%)
  blocking collectives  16.2 us (21%)
  waiting for transfers between devices  15.6 us (21%)
  Pallas kernels  12.9 us (17%)
  between operations  0.77 us (1%)
    all_to_all x1, blocking collectives, on_device(): q_own = lax.all_to_all(entering, PLANE, 0, 0)  16.2 us
    ppermute x7, starting transfers between devices, moved_by(): return lax.ppermute(array, axis, [(i, (i + by) % n) for i in range(n)])  12.5 us
    all_to_all x1, starting transfers between devices, on_device(): maps = lax.all_to_all(pieces, PLANE, 0, 0).reshape(plane * PIECE, LANES)  10.2 us
    all_to_all x1, waiting for transfers between devices, on_device(): maps = lax.all_to_all(pieces, PLANE, 0, 0).reshape(plane * PIECE, LANES)  7.83 us
    ppermute x2, starting transfers between devices, moved_down(): return lax.ppermute(array, ALL, [(i, i - 1) for i in range(1, count)])  7.51 us
    ppermute x2, waiting for transfers between devices, moved_down(): return lax.ppermute(array, ALL, [(i, i - 1) for i in range(1, count)])  5.37 us
    pallas_call x1, Pallas kernels, on_device(): pl.pallas_call(first_kernel, out_shape=(square, pltpu.VMEM((layers, batch...  4.25 us
    pallas_call x1, Pallas kernels, on_device(): pl.pallas_call(final_kernel, out_shape=(jax.ShapeDtypeStruct((1, batch, w...  3.01 us
  transfers between devices with their start and end apart: 10, of which 4 were waited for; matrix products, arithmetic and copies ran while one was open for 0% of the time, Pallas kernels for 4%

profile of v3, /device:TPU:1, one launch (start us, length us, event | category | flops | bytes accessed | tf_op | source)
XLA Modules:
  0.0 75.6 jit_solution(2076136303507535579)
XLA Ops:
  0.6 0.0 copy-start
  0.6 4.2 %first.1 = (f32[128,1024]{1,0:T(8,128)S(1)}, f32[2,128,1024]{2,1,0:T(8,128)S(1)}, bf16[2,1024,1024]{2,1,0:T(8,128)(2,1)S(1)}) custom-call(bf16[2,1024,1024]{2,1,0:T(8,128)(2,1)} %w.3, f32[2,1024]{1,0:T(2,128)} %b.1, bf16[2,128,1024]{2,1,0:T(8,128)(2,1)} %s.3, f32[1,128,1024]{2,1,0:T(8,128)} %g.3), custom_call_target="tpu_custom_call" | custom-call | tf_op jit(solution)/shard_map/first/pallas_call | solution.py:345
  4.9 5.2 %collective-permute-start = (f32[128,1024]{1,0:T(8,128)S(1)}, f32[128,1024]{1,0:T(8,128)S(1)}, u32[]{:S(2)}, u32[]{:S(2)}) collective-permute-start(f32[128,1024]{1,0:T(8,128)S(1)} %get-tuple-element.20.moved), channel_id=1, source_target_pairs={{1,0},{2,1},{3,2},{4,3},{5,4},{6,5},{7,6},{8,7},{9,8},{10,9},{11,1... | collective-permute-start | bytes 1572872 | tf_op jit(solution)/shard_map/ppermute | solution.py:331
  10.1 0.0 copy-done
  10.1 0.1 collective-permute-start.1
  10.2 1.2 %collective-permute-done.1.rup = f32[1,1024]{1,0:T(1,128)S(1)} collective-permute-done((f32[1,1024]{1,0:T(1,128)S(1)}, f32[1,1024]{1,0:T(1,128)S(1)}, u32[]{:S(2)}, u32[]{:S(2)}) %collective-permute-start.1) | collective-permute-done | bytes 4128 | tf_op jit(solution)/shard_map/ppermute | solution.py:326
  11.3 5.4 %collective-permute-done.above = f32[128,1024]{1,0:T(8,128)S(1)} collective-permute-done((f32[128,1024]{1,0:T(8,128)S(1)}, f32[128,1024]{1,0:T(8,128)S(1)}, u32[]{:S(2)}, u32[]{:S(2)}) %collective-permute-start) | collective-permute-done | bytes 524320 | tf_op jit(solution)/shard_map/ppermute | solution.py:331
  16.7 1.7 %second.1 = (f32[128,1024]{1,0:T(8,128)}, f32[128,1024]{1,0:T(8,128)S(1)}, f32[128,512]{1,0:T(8,128)S(1)}, f32[136,512]{1,0:T(8,128)S(1)}, f32[128,512]{1,0:T(8,128)S(1)}) custom-call(f32[1,128,1024]{2,1,0:T(8,128)} %g.3, f32[128,1024]{1,0:T(8,128)} %og.5, f32[128,1024]{1,0:T(8,128)S(1)} %collective-permute-done.above, ...), custom_call_target="tpu_custom_call" | custom-call | tf_op jit(solution)/shard_map/second/pallas_call | solution.py:370
  18.4 3.7 %collective-permute-start.2 = (f32[136,512]{1,0:T(8,128)S(1)}, f32[136,512]{1,0:T(8,128)S(1)}, u32[]{:S(2)}, u32[]{:S(2)}) collective-permute-start(f32[136,512]{1,0:T(8,128)S(1)} %get-tuple-element.24), channel_id=1, source_target_pairs={{0,1},{1,0},{2,3},{3,2},{4,5},{5,4},{6,7},{7,6},{8,9},{9,8},{10,11... | collective-permute-start | bytes 835592 | tf_op jit(solution)/shard_map/ppermute | solution.py:326
  22.1 1.2 %collective-permute-done.2.got = f32[136,512]{1,0:T(8,128)S(1)} collective-permute-done((f32[136,512]{1,0:T(8,128)S(1)}, f32[136,512]{1,0:T(8,128)S(1)}, u32[]{:S(2)}, u32[]{:S(2)}) %collective-permute-start.2) | collective-permute-done | bytes 278560 | tf_op jit(solution)/shard_map/ppermute | solution.py:326
  23.3 0.8 %chip.1 = f32[544,128]{1,0:T(8,128)} custom-call(f32[128,512]{1,0:T(8,128)S(1)} %get-tuple-element.23.keep, f32[136,512]{1,0:T(8,128)S(1)} %collective-permute-done.2.got, f32[1,1024]{1,0:T(1,128)S(1)} %copy-done, f32[1,1024]{1,0:T(1,128)S(1)} %collective-permute-done.1.rup), custom_call_target="tpu_custom_call" | custom-call | tf_op jit(solution)/shard_map/chip/pallas_call | solution.py:387
  24.1 10.2 %all-to-all-start = ((f32[32,17,1,128]{3,2,1,0:T(1,128)}), f32[32,17,1,128]{3,2,1,0:T(1,128)S(1)}, u32[]{:S(2)}, u32[]{:S(2)}) async-start(f32[32,17,1,128]{3,2,1,0:T(1,128)} %bitcast), calls=%async_computation | async-start | bytes 557056 | tf_op jit(solution)/shard_map/all_to_all | solution.py:396
  34.2 2.3 %collective-permute-start.6 = (f32[128,1024]{1,0:T(8,128)S(1)}, f32[128,1024]{1,0:T(8,128)S(1)}, u32[]{:S(2)}, u32[]{:S(2)}) collective-permute-start(f32[128,1024]{1,0:T(8,128)S(1)} %get-tuple-element.28), channel_id=1, source_target_pairs={{1,0},{2,1},{3,2},{4,3},{5,4},{6,5},{7,6},{8,7},{9,8},{10,9},{11,1... | collective-permute-start | bytes 1572872 | tf_op jit(solution)/shard_map/ppermute | solution.py:331
  36.6 0.1 collective-permute-start.7
  36.7 7.8 %all-to-all-done = f32[32,17,1,128]{3,2,1,0:T(1,128)S(1)} async-done(((f32[32,17,1,128]{3,2,1,0:T(1,128)}), f32[32,17,1,128]{3,2,1,0:T(1,128)S(1)}, u32[]{:S(2)}, u32[]{:S(2)}) %all-to-all-start) | async-done | bytes 278560 | tf_op jit(solution)/shard_map/all_to_all | solution.py:396
  44.5 0.1 plane.1
  44.6 1.3 %collective-permute-start.5 = (f32[24,128]{1,0:T(8,128)S(1)}, f32[24,128]{1,0:T(8,128)S(1)}, u32[]{:S(2)}, u32[]{:S(2)}) collective-permute-start(f32[24,128]{1,0:T(8,128)S(1)} %get-tuple-element.27.after), channel_id=1, source_target_pairs={{0,64},{64,128},{128,192},{192,0},{1,65},{65,129},{129,193},{193,1... | collective-permute-start | bytes 36872 | tf_op jit(solution)/shard_map/ppermute | solution.py:326
  45.9 1.6 %collective-permute-start.4 = (f32[24,128]{1,0:T(8,128)S(1)}, f32[24,128]{1,0:T(8,128)S(1)}, u32[]{:S(2)}, u32[]{:S(2)}) collective-permute-start(f32[24,128]{1,0:T(8,128)S(1)} %get-tuple-element.27.after), channel_id=1, source_target_pairs={{0,128},{64,192},{128,0},{192,64},{1,129},{65,193},{129,1},{193,65... | collective-permute-start | bytes 36872 | tf_op jit(solution)/shard_map/ppermute | solution.py:326
  47.5 2.0 %collective-permute-start.3 = (f32[24,128]{1,0:T(8,128)S(1)}, f32[24,128]{1,0:T(8,128)S(1)}, u32[]{:S(2)}, u32[]{:S(2)}) collective-permute-start(f32[24,128]{1,0:T(8,128)S(1)} %get-tuple-element.27.after), channel_id=1, source_target_pairs={{0,192},{64,0},{128,64},{192,128},{1,193},{65,1},{129,65},{193,129... | collective-permute-start | bytes 36872 | tf_op jit(solution)/shard_map/ppermute | solution.py:326
  49.5 1.9 %fetch.1 = (f32[128,1024]{1,0:T(8,128)S(1)}, bf16[1,1024,1024]{2,1,0:T(8,128)(2,1)S(1)}, bf16[2,128,1024]{2,1,0:T(8,128)(2,1)S(1)}) custom-call(f32[128,1024]{1,0:T(8,128)} %get-tuple-element.30.first, bf16[2,1024,1024]{2,1,0:T(8,128)(2,1)} %w.3, bf16[2,128,1024]{2,1,0:T(8,128)(2,1)} %s.3, f32[24,128]{1,0:T(8,128)S(1)} %get-tuple-element.27.after), custom_call_target="tpu_custom_call" | custom-call | bytes 6291456 | tf_op jit(solution)/shard_map/fetch/pallas_call | solution.py:412
  51.4 0.0 collective-permute-done.7.rest
  51.5 0.0 collective-permute-done.6.res.res_in
  51.5 0.0 collective-permute-done.5.three
  51.5 0.0 collective-permute-done.4.two
  51.5 0.0 collective-permute-done.3.one
  51.5 16.2 %all_to_all.10.q_own = f32[32,16,128]{2,1,0:T(8,128)S(1)} all-to-all(f32[32,16,128]{2,1,0:T(8,128)S(1)} %scan.1), channel_id=1, replica_groups=mesh['x'=4,'y'=4,'z'=8,'c'=2] {'y','z'}, dimensions={0} | all-to-all | bytes 524288 | tf_op jit(solution)/shard_map/all_to_all | solution.py:435
  67.7 3.7 %collective-permute-start.8 = (f32[32,16,128]{2,1,0:T(8,128)S(1)}, f32[32,16,128]{2,1,0:T(8,128)S(1)}, u32[]{:S(2)}, u32[]{:S(2)}) collective-permute-start(f32[32,16,128]{2,1,0:T(8,128)S(1)} %all_to_all.10.q_own), channel_id=1, source_target_pairs={{0,1},{1,0},{2,3},{3,2},{4,5},{5,4},{6,7},{7,6},{8,9},{9,8},{10,11... | collective-permute-start | bytes 786440 | tf_op jit(solution)/shard_map/ppermute | solution.py:326
  71.4 1.1 %own.1 = (f32[128,512]{1,0:T(8,128)S(1)}, bf16[1024,512]{1,0:T(8,128)(2,1)S(1)}, f32[128,1024]{1,0:T(8,128)S(1)}) custom-call(f32[32,16,128]{2,1,0:T(8,128)S(1)} %all_to_all.10.q_own, f32[136,512]{1,0:T(8,128)S(1)} %collective-permute-done.2.got, f32[1,1024]{1,0:T(1,128)S(1)} %copy-done, f32[2,128,1024]{2,1,0:T(8,128)S(1)} %get-tuple-element.21.slopes, ...), custom_call_target="tpu_custom_call" | custom-call | flops 140000000 | bytes 4194304 | tf_op jit(solution)/shard_map/own/pallas_call | solution.py:437
  72.5 0.0 collective-permute-done.8.q_other
  72.6 3.0 %final.1 = (f32[1,128,1024]{2,1,0:T(8,128)}, bf16[2,1024,1024]{2,1,0:T(8,128)(2,1)}, f32[1,128,1024]{2,1,0:T(8,128)}) custom-call(f32[32,16,128]{2,1,0:T(8,128)S(1)} %collective-permute-done.8.q_other, f32[128,512]{1,0:T(8,128)S(1)} %collective-permute-done.7.rest, f32[1,1024]{1,0:T(1,128)S(1)} %copy-done, f32[2,128,1024]{2,1,0:T(8,128)S(1)} %get-tuple-element.21.slopes, ...), custom_call_target="tpu_custom_call" | custom-call | tf_op jit(solution)/shard_map/final/pallas_call | solution.py:451
  (1 shorter events, 0.0 us)
Async XLA Ops:
  0.6 9.4 %copy-start = (f32[1,1024]{1,0:T(1,128)S(1)}, f32[1,1024]{1,0:T(1,128)}, u32[]{:S(2)}) copy-start(f32[1,1024]{1,0:T(1,128)} %rate.5) | copy-start | bytes 12292
  4.9 11.8 %collective-permute-start = (f32[128,1024]{1,0:T(8,128)S(1)}, f32[128,1024]{1,0:T(8,128)S(1)}, u32[]{:S(2)}, u32[]{:S(2)}) collective-permute-start(f32[128,1024]{1,0:T(8,128)S(1)} %get-tuple-element.20.moved), channel_id=1, source_target_pairs={{1,0},{2,1},{3,2},{4,3},{5,4},{6,5},{7,6},{8,7},{9,8},{10,9},{11,1... | collective-permute-start | bytes 1572872 | tf_op jit(solution)/shard_map/ppermute | solution.py:331
  10.1 1.2 %collective-permute-start.1 = (f32[1,1024]{1,0:T(1,128)S(1)}, f32[1,1024]{1,0:T(1,128)S(1)}, u32[]{:S(2)}, u32[]{:S(2)}) collective-permute-start(f32[1,1024]{1,0:T(1,128)S(1)} %copy-done), channel_id=1, source_target_pairs={{0,1},{1,2},{2,3},{3,4},{4,5},{5,6},{6,7},{7,8},{8,9},{9,10},{10,1... | collective-permute-start | bytes 12296 | tf_op jit(solution)/shard_map/ppermute | solution.py:326
  18.4 4.9 %collective-permute-start.2 = (f32[136,512]{1,0:T(8,128)S(1)}, f32[136,512]{1,0:T(8,128)S(1)}, u32[]{:S(2)}, u32[]{:S(2)}) collective-permute-start(f32[136,512]{1,0:T(8,128)S(1)} %get-tuple-element.24), channel_id=1, source_target_pairs={{0,1},{1,0},{2,3},{3,2},{4,5},{5,4},{6,7},{7,6},{8,9},{9,8},{10,11... | collective-permute-start | bytes 835592 | tf_op jit(solution)/shard_map/ppermute | solution.py:326
  24.1 20.4 %all-to-all-start = ((f32[32,17,1,128]{3,2,1,0:T(1,128)}), f32[32,17,1,128]{3,2,1,0:T(1,128)S(1)}, u32[]{:S(2)}, u32[]{:S(2)}) async-start(f32[32,17,1,128]{3,2,1,0:T(1,128)} %bitcast), calls=%async_computation | async-start | bytes 557056 | tf_op jit(solution)/shard_map/all_to_all | solution.py:396
  34.2 17.2 %collective-permute-start.6 = (f32[128,1024]{1,0:T(8,128)S(1)}, f32[128,1024]{1,0:T(8,128)S(1)}, u32[]{:S(2)}, u32[]{:S(2)}) collective-permute-start(f32[128,1024]{1,0:T(8,128)S(1)} %get-tuple-element.28), channel_id=1, source_target_pairs={{1,0},{2,1},{3,2},{4,3},{5,4},{6,5},{7,6},{8,7},{9,8},{10,9},{11,1... | collective-permute-start | bytes 1572872 | tf_op jit(solution)/shard_map/ppermute | solution.py:331
  36.6 14.9 %collective-permute-start.7 = (f32[128,512]{1,0:T(8,128)S(1)}, f32[128,512]{1,0:T(8,128)S(1)}, u32[]{:S(2)}, u32[]{:S(2)}) collective-permute-start(f32[128,512]{1,0:T(8,128)S(1)} %get-tuple-element.29), channel_id=1, source_target_pairs={{0,1},{1,0},{2,3},{3,2},{4,5},{5,4},{6,7},{7,6},{8,9},{9,8},{10,11... | collective-permute-start | bytes 786440 | tf_op jit(solution)/shard_map/ppermute | solution.py:326
  44.6 6.9 %collective-permute-start.5 = (f32[24,128]{1,0:T(8,128)S(1)}, f32[24,128]{1,0:T(8,128)S(1)}, u32[]{:S(2)}, u32[]{:S(2)}) collective-permute-start(f32[24,128]{1,0:T(8,128)S(1)} %get-tuple-element.27.after), channel_id=1, source_target_pairs={{0,64},{64,128},{128,192},{192,0},{1,65},{65,129},{129,193},{193,1... | collective-permute-start | bytes 36872 | tf_op jit(solution)/shard_map/ppermute | solution.py:326
  45.9 5.6 %collective-permute-start.4 = (f32[24,128]{1,0:T(8,128)S(1)}, f32[24,128]{1,0:T(8,128)S(1)}, u32[]{:S(2)}, u32[]{:S(2)}) collective-permute-start(f32[24,128]{1,0:T(8,128)S(1)} %get-tuple-element.27.after), channel_id=1, source_target_pairs={{0,128},{64,192},{128,0},{192,64},{1,129},{65,193},{129,1},{193,65... | collective-permute-start | bytes 36872 | tf_op jit(solution)/shard_map/ppermute | solution.py:326
  47.5 4.0 %collective-permute-start.3 = (f32[24,128]{1,0:T(8,128)S(1)}, f32[24,128]{1,0:T(8,128)S(1)}, u32[]{:S(2)}, u32[]{:S(2)}) collective-permute-start(f32[24,128]{1,0:T(8,128)S(1)} %get-tuple-element.27.after), channel_id=1, source_target_pairs={{0,192},{64,0},{128,64},{192,128},{1,193},{65,1},{129,65},{193,129... | collective-permute-start | bytes 36872 | tf_op jit(solution)/shard_map/ppermute | solution.py:326
  67.7 4.8 %collective-permute-start.8 = (f32[32,16,128]{2,1,0:T(8,128)S(1)}, f32[32,16,128]{2,1,0:T(8,128)S(1)}, u32[]{:S(2)}, u32[]{:S(2)}) collective-permute-start(f32[32,16,128]{2,1,0:T(8,128)S(1)} %all_to_all.10.q_own), channel_id=1, source_target_pairs={{0,1},{1,0},{2,3},{3,2},{4,5},{5,4},{6,7},{7,6},{8,9},{9,8},{10,11... | collective-permute-start | bytes 786440 | tf_op jit(solution)/shard_map/ppermute | solution.py:326

commit v4 on v3

--- a/solution.py
+++ b/solution.py
@@ -220,19 +220,7 @@
         extra[...] = jnp.zeros_like(extra)
 
 
-def half_product(core0, out, q, wv, k):
-    top, half = wv.shape[0] - 1, q.shape[1]
-
-    @pl.when(core0 == (k == 0))
-    def _():
-        out[...] = times_transposed(q[...], wv[top, :, :half])
-
-    @pl.when(core0 != (k == 0))
-    def _():
-        out[...] = times_transposed(q[...], wv[top, :, half:])
-
-
-def own_kernel(q_own, got, rate, slopes, first, wv, sv, og, lam_h, g_h, part, q_h, extra, sem):
+def own_kernel(q_own, got, rate, slopes, first, sv, og, lam_h, q_h, g_h, extra, sem):
     core0 = lax.axis_index("c") == 0
     batch, half = lam_h.shape
     l = slopes.shape[0] - 1
@@ -244,15 +232,14 @@
     lam_h[...] = lam
     q = (lam * jnp.where(core0, slopes[l, :, :half], slopes[l, :, half:])).astype(BF16)
     q_h[...] = q
-    half_product(core0, part, q_h, wv, 0)
     for n in range(g_h.shape[0] // PART):
         rows = slice(n * PART, (n + 1) * PART)
         g_h[rows, :] = (transposed_times(sv[l, :, rows], q) * (0.5 / batch)).astype(BF16)
 
 
 def final_kernel(
-    q_other, rest, rate, slopes, first, wv, sv, lam_h, g_h, part, og, res_in,
-    corrected, grads, res, lam_v, q_o, more, extra, gbuf, g_o, sem, gsem,
+    q_other, rest, rate, slopes, first, wv, sv, lam_h, q_h, g_h, og, res_in,
+    corrected, grads, res, lam_v, q_v, extra, gbuf, g_o, sem, gsem,
 ):
     top = is_top()
     core0 = lax.axis_index("c") == 0
@@ -287,21 +274,21 @@
     err = jnp.where(core0, f[:, half:] * e + rest[...], e + extra[:, :half])
     other = jnp.where(core0, first[:, half:], first[:, :half]) + err
     q = (other * jnp.where(core0, slopes[l, :, half:], slopes[l, :, :half])).astype(BF16)
-    q_o[...] = q
-    half_product(core0, more, q_o, wv, 1)
     for n in range(width // PART):
         rows = slice(n * PART, (n + 1) * PART)
         g_o[rows, :] = (transposed_times(sv[l, :, rows], q) * (0.5 / batch)).astype(BF16)
     columns(g_o, 1)
-    own = lam_h[...]
+    own, q_own = lam_h[...], q_h[...]
     lam_v[:, :half] = jnp.where(core0, own, other)
     lam_v[:, half:] = jnp.where(core0, other, own)
+    q_v[:, :half] = jnp.where(core0, q_own, q)
+    q_v[:, half:] = jnp.where(core0, q, q_own)
     keep = pltpu.make_async_copy(lam_v, corrected.at[0], sem.at[2])
     keep.start()
     copies = []
-    lam, product = lam_v[...], part[...] + more[...]
+    lam, q = lam_v[...], q_v[...]
     for k in reversed(range(l)):
-        lam = lam + 0.5 * product
+        lam = lam + 0.5 * times_transposed(q, wv[k])
         q = (lam * slopes[k]).astype(BF16)
         for n in range(width // PART):
             rows = slice(n * PART, (n + 1) * PART)
@@ -311,8 +298,6 @@
             copy = pltpu.make_async_copy(gbuf.at[k, pl.ds(n * PART, PART)], there, gsem.at[k, n])
             copy.start()
             copies.append(copy)
-        if k:
-            product = times_transposed(q, wv[k - 1])
     keep.wait()
     pltpu.make_async_copy(g_h, grads.at[l, :, low], sem.at[0]).wait()
     pltpu.make_async_copy(g_o, grads.at[l, :, low], sem.at[1]).wait()
@@ -434,20 +419,20 @@
     )(terms, factors, *higher, got_res, got_rest, first, wv, sv)
     q_own = lax.all_to_all(entering, PLANE, 0, 0)
     q_other = moved_by(q_own, "c", 1)
-    lam_h, g_h, part = pl.pallas_call(
+    lam_h, q_h, g_h = pl.pallas_call(
         own_kernel,
         out_shape=(
             pltpu.VMEM((batch, half), F32),
+            pltpu.VMEM((batch, half), BF16),
             pltpu.VMEM((width, half), BF16),
-            pltpu.VMEM((batch, width), F32),
-        ),
-        in_specs=[VMEM] * 7 + [HBM],
+        ),
+        in_specs=[VMEM] * 6 + [HBM],
         out_specs=(VMEM,) * 3,
-        scratch_shapes=[pltpu.VMEM((batch, half), BF16), pltpu.VMEM((batch, width), F32), dma((1,))],
+        scratch_shapes=[pltpu.VMEM((batch, width), F32), dma((1,))],
         compiler_params=params(8),
         cost_estimate=pl.CostEstimate(flops=140000000, bytes_accessed=4 * MIB, transcendentals=0),
         name="own",
-    )(q_own, got, coarse_rate, slopes, first, wv, sv, output_grad)
+    )(q_own, got, coarse_rate, slopes, first, sv, output_grad)
     return pl.pallas_call(
         final_kernel,
         out_shape=(
@@ -459,8 +444,7 @@
         out_specs=(HBM,) * 3,
         scratch_shapes=[
             pltpu.VMEM((batch, width), F32),
-            pltpu.VMEM((batch, half), BF16),
-            pltpu.VMEM((batch, width), F32),
+            pltpu.VMEM((batch, width), BF16),
             pltpu.VMEM((batch, width), F32),
             pltpu.VMEM((layers - 1, width, width), BF16),
             pltpu.VMEM((width, half), BF16),
@@ -471,7 +455,7 @@
         name="final",
     )(
         q_other, got_rest, coarse_rate, slopes, first, wv, sv,
-        in_vmem(lam_h), in_vmem(g_h), in_vmem(part), output_grad, got_res,
+        in_vmem(lam_h), in_vmem(q_h), in_vmem(g_h), output_grad, got_res,
     )
 
 

time: 75.9 us -> 75.7 us (level)
  Pallas kernels: 12.9 us -> 12.1 us
  transfers between devices with their start and end apart: 10 -> 10, of which waited for: 4 -> 5; matrix products, arithmetic and copies ran while one was open for 0% -> 0% of each run, Pallas kernels for 4% -> 3%
where the time goes in v4:
time: 75.7 us; the launch traced here: 75.4 us
  starting transfers between devices  30.1 us (40%)
  blocking collectives  16.2 us (21%)
  waiting for transfers between devices  16.1 us (21%)
  Pallas kernels  12.1 us (16%)
  between operations  0.77 us (1%)
    all_to_all x1, blocking collectives, on_device(): q_own = lax.all_to_all(entering, PLANE, 0, 0)  16.2 us
    ppermute x7, starting transfers between devices, moved_by(): return lax.ppermute(array, axis, [(i, (i + by) % n) for i in range(n)])  12.5 us
    all_to_all x1, starting transfers between devices, on_device(): maps = lax.all_to_all(pieces, PLANE, 0, 0).reshape(plane * PIECE, LANES)  10.2 us
    all_to_all x1, waiting for transfers between devices, on_device(): maps = lax.all_to_all(pieces, PLANE, 0, 0).reshape(plane * PIECE, LANES)  7.83 us
    ppermute x2, starting transfers between devices, moved_down(): return lax.ppermute(array, ALL, [(i, i - 1) for i in range(1, count)])  7.51 us
    ppermute x2, waiting for transfers between devices, moved_down(): return lax.ppermute(array, ALL, [(i, i - 1) for i in range(1, count)])  5.37 us
    pallas_call x1, Pallas kernels, on_device(): pl.pallas_call(first_kernel, out_shape=(square, pltpu.VMEM((layers, batch...  4.25 us
    ppermute x7, waiting for transfers between devices, moved_by(): return lax.ppermute(array, axis, [(i, (i + by) % n) for i in range(n)])  2.94 us
  transfers between devices with their start and end apart: 10, of which 5 were waited for; matrix products, arithmetic and copies ran while one was open for 0% of the time, Pallas kernels for 3%

profile of v4, /device:TPU:1, one launch (start us, length us, event | category | flops | bytes accessed | tf_op | source)
XLA Modules:
  0.0 75.4 jit_solution(17815619661913129141)
XLA Ops:
  0.6 0.0 copy-start
  0.6 4.2 %first.1 = (f32[128,1024]{1,0:T(8,128)S(1)}, f32[2,128,1024]{2,1,0:T(8,128)S(1)}, bf16[2,1024,1024]{2,1,0:T(8,128)(2,1)S(1)}) custom-call(bf16[2,1024,1024]{2,1,0:T(8,128)(2,1)} %w.3, f32[2,1024]{1,0:T(2,128)} %b.1, bf16[2,128,1024]{2,1,0:T(8,128)(2,1)} %s.3, f32[1,128,1024]{2,1,0:T(8,128)} %g.3), custom_call_target="tpu_custom_call" | custom-call | tf_op jit(solution)/shard_map/first/pallas_call | solution.py:330
  4.9 5.2 %collective-permute-start = (f32[128,1024]{1,0:T(8,128)S(1)}, f32[128,1024]{1,0:T(8,128)S(1)}, u32[]{:S(2)}, u32[]{:S(2)}) collective-permute-start(f32[128,1024]{1,0:T(8,128)S(1)} %get-tuple-element.20.moved), channel_id=1, source_target_pairs={{1,0},{2,1},{3,2},{4,3},{5,4},{6,5},{7,6},{8,7},{9,8},{10,9},{11,1... | collective-permute-start | bytes 1572872 | tf_op jit(solution)/shard_map/ppermute | solution.py:316
  10.1 0.0 copy-done
  10.1 0.1 collective-permute-start.1
  10.2 1.2 %collective-permute-done.1.rup = f32[1,1024]{1,0:T(1,128)S(1)} collective-permute-done((f32[1,1024]{1,0:T(1,128)S(1)}, f32[1,1024]{1,0:T(1,128)S(1)}, u32[]{:S(2)}, u32[]{:S(2)}) %collective-permute-start.1) | collective-permute-done | bytes 4128 | tf_op jit(solution)/shard_map/ppermute | solution.py:311
  11.3 5.4 %collective-permute-done.above = f32[128,1024]{1,0:T(8,128)S(1)} collective-permute-done((f32[128,1024]{1,0:T(8,128)S(1)}, f32[128,1024]{1,0:T(8,128)S(1)}, u32[]{:S(2)}, u32[]{:S(2)}) %collective-permute-start) | collective-permute-done | bytes 524320 | tf_op jit(solution)/shard_map/ppermute | solution.py:316
  16.7 1.7 %second.1 = (f32[128,1024]{1,0:T(8,128)}, f32[128,1024]{1,0:T(8,128)S(1)}, f32[128,512]{1,0:T(8,128)S(1)}, f32[136,512]{1,0:T(8,128)S(1)}, f32[128,512]{1,0:T(8,128)S(1)}) custom-call(f32[1,128,1024]{2,1,0:T(8,128)} %g.3, f32[128,1024]{1,0:T(8,128)} %og.5, f32[128,1024]{1,0:T(8,128)S(1)} %collective-permute-done.above, ...), custom_call_target="tpu_custom_call" | custom-call | tf_op jit(solution)/shard_map/second/pallas_call | solution.py:355
  18.4 3.7 %collective-permute-start.2 = (f32[136,512]{1,0:T(8,128)S(1)}, f32[136,512]{1,0:T(8,128)S(1)}, u32[]{:S(2)}, u32[]{:S(2)}) collective-permute-start(f32[136,512]{1,0:T(8,128)S(1)} %get-tuple-element.24), channel_id=1, source_target_pairs={{0,1},{1,0},{2,3},{3,2},{4,5},{5,4},{6,7},{7,6},{8,9},{9,8},{10,11... | collective-permute-start | bytes 835592 | tf_op jit(solution)/shard_map/ppermute | solution.py:311
  22.1 1.2 %collective-permute-done.2.got = f32[136,512]{1,0:T(8,128)S(1)} collective-permute-done((f32[136,512]{1,0:T(8,128)S(1)}, f32[136,512]{1,0:T(8,128)S(1)}, u32[]{:S(2)}, u32[]{:S(2)}) %collective-permute-start.2) | collective-permute-done | bytes 278560 | tf_op jit(solution)/shard_map/ppermute | solution.py:311
  23.3 0.8 %chip.1 = f32[544,128]{1,0:T(8,128)} custom-call(f32[128,512]{1,0:T(8,128)S(1)} %get-tuple-element.23.keep, f32[136,512]{1,0:T(8,128)S(1)} %collective-permute-done.2.got, f32[1,1024]{1,0:T(1,128)S(1)} %copy-done, f32[1,1024]{1,0:T(1,128)S(1)} %collective-permute-done.1.rup), custom_call_target="tpu_custom_call" | custom-call | tf_op jit(solution)/shard_map/chip/pallas_call | solution.py:372
  24.1 10.2 %all-to-all-start = ((f32[32,17,1,128]{3,2,1,0:T(1,128)}), f32[32,17,1,128]{3,2,1,0:T(1,128)S(1)}, u32[]{:S(2)}, u32[]{:S(2)}) async-start(f32[32,17,1,128]{3,2,1,0:T(1,128)} %bitcast), calls=%async_computation | async-start | bytes 557056 | tf_op jit(solution)/shard_map/all_to_all | solution.py:381
  34.2 2.3 %collective-permute-start.6 = (f32[128,1024]{1,0:T(8,128)S(1)}, f32[128,1024]{1,0:T(8,128)S(1)}, u32[]{:S(2)}, u32[]{:S(2)}) collective-permute-start(f32[128,1024]{1,0:T(8,128)S(1)} %get-tuple-element.28), channel_id=1, source_target_pairs={{1,0},{2,1},{3,2},{4,3},{5,4},{6,5},{7,6},{8,7},{9,8},{10,9},{11,1... | collective-permute-start | bytes 1572872 | tf_op jit(solution)/shard_map/ppermute | solution.py:316
  36.6 0.1 collective-permute-start.7
  36.7 7.8 %all-to-all-done = f32[32,17,1,128]{3,2,1,0:T(1,128)S(1)} async-done(((f32[32,17,1,128]{3,2,1,0:T(1,128)}), f32[32,17,1,128]{3,2,1,0:T(1,128)S(1)}, u32[]{:S(2)}, u32[]{:S(2)}) %all-to-all-start) | async-done | bytes 278560 | tf_op jit(solution)/shard_map/all_to_all | solution.py:381
  44.5 0.1 plane.1
  44.6 1.3 %collective-permute-start.5 = (f32[24,128]{1,0:T(8,128)S(1)}, f32[24,128]{1,0:T(8,128)S(1)}, u32[]{:S(2)}, u32[]{:S(2)}) collective-permute-start(f32[24,128]{1,0:T(8,128)S(1)} %get-tuple-element.27.after), channel_id=1, source_target_pairs={{0,64},{64,128},{128,192},{192,0},{1,65},{65,129},{129,193},{193,1... | collective-permute-start | bytes 36872 | tf_op jit(solution)/shard_map/ppermute | solution.py:311
  45.9 1.6 %collective-permute-start.4 = (f32[24,128]{1,0:T(8,128)S(1)}, f32[24,128]{1,0:T(8,128)S(1)}, u32[]{:S(2)}, u32[]{:S(2)}) collective-permute-start(f32[24,128]{1,0:T(8,128)S(1)} %get-tuple-element.27.after), channel_id=1, source_target_pairs={{0,128},{64,192},{128,0},{192,64},{1,129},{65,193},{129,1},{193,65... | collective-permute-start | bytes 36872 | tf_op jit(solution)/shard_map/ppermute | solution.py:311
  47.5 2.0 %collective-permute-start.3 = (f32[24,128]{1,0:T(8,128)S(1)}, f32[24,128]{1,0:T(8,128)S(1)}, u32[]{:S(2)}, u32[]{:S(2)}) collective-permute-start(f32[24,128]{1,0:T(8,128)S(1)} %get-tuple-element.27.after), channel_id=1, source_target_pairs={{0,192},{64,0},{128,64},{192,128},{1,193},{65,1},{129,65},{193,129... | collective-permute-start | bytes 36872 | tf_op jit(solution)/shard_map/ppermute | solution.py:311
  49.5 1.9 %fetch.1 = (f32[128,1024]{1,0:T(8,128)S(1)}, bf16[1,1024,1024]{2,1,0:T(8,128)(2,1)S(1)}, bf16[2,128,1024]{2,1,0:T(8,128)(2,1)S(1)}) custom-call(f32[128,1024]{1,0:T(8,128)} %get-tuple-element.30.first, bf16[2,1024,1024]{2,1,0:T(8,128)(2,1)} %w.3, bf16[2,128,1024]{2,1,0:T(8,128)(2,1)} %s.3, f32[24,128]{1,0:T(8,128)S(1)} %get-tuple-element.27.after), custom_call_target="tpu_custom_call" | custom-call | bytes 6291456 | tf_op jit(solution)/shard_map/fetch/pallas_call | solution.py:397
  51.4 0.0 collective-permute-done.7.rest
  51.5 0.0 collective-permute-done.6.res.res_in
  51.5 0.0 collective-permute-done.5.three
  51.5 0.0 collective-permute-done.4.two
  51.5 0.0 collective-permute-done.3.one
  51.5 16.2 %all_to_all.10.q_own = f32[32,16,128]{2,1,0:T(8,128)S(1)} all-to-all(f32[32,16,128]{2,1,0:T(8,128)S(1)} %scan.1), channel_id=1, replica_groups=mesh['x'=4,'y'=4,'z'=8,'c'=2] {'y','z'}, dimensions={0} | all-to-all | bytes 524288 | tf_op jit(solution)/shard_map/all_to_all | solution.py:420
  67.7 3.7 %collective-permute-start.8 = (f32[32,16,128]{2,1,0:T(8,128)S(1)}, f32[32,16,128]{2,1,0:T(8,128)S(1)}, u32[]{:S(2)}, u32[]{:S(2)}) collective-permute-start(f32[32,16,128]{2,1,0:T(8,128)S(1)} %all_to_all.10.q_own), channel_id=1, source_target_pairs={{0,1},{1,0},{2,3},{3,2},{4,5},{5,4},{6,7},{7,6},{8,9},{9,8},{10,11... | collective-permute-start | bytes 786440 | tf_op jit(solution)/shard_map/ppermute | solution.py:311
  71.4 0.6 own.1
  72.0 0.6 collective-permute-done.8.q_other
  72.6 2.8 %final.1 = (f32[1,128,1024]{2,1,0:T(8,128)}, bf16[2,1024,1024]{2,1,0:T(8,128)(2,1)}, f32[1,128,1024]{2,1,0:T(8,128)}) custom-call(f32[32,16,128]{2,1,0:T(8,128)S(1)} %collective-permute-done.8.q_other, f32[128,512]{1,0:T(8,128)S(1)} %collective-permute-done.7.rest, f32[1,1024]{1,0:T(1,128)S(1)} %copy-done, f32[2,128,1024]{2,1,0:T(8,128)S(1)} %get-tuple-element.21.slopes, ...), custom_call_target="tpu_custom_call" | custom-call | tf_op jit(solution)/shard_map/final/pallas_call | solution.py:436
  (1 shorter events, 0.0 us)
Async XLA Ops:
  0.6 9.4 %copy-start = (f32[1,1024]{1,0:T(1,128)S(1)}, f32[1,1024]{1,0:T(1,128)}, u32[]{:S(2)}) copy-start(f32[1,1024]{1,0:T(1,128)} %rate.5) | copy-start | bytes 12292
  4.9 11.8 %collective-permute-start = (f32[128,1024]{1,0:T(8,128)S(1)}, f32[128,1024]{1,0:T(8,128)S(1)}, u32[]{:S(2)}, u32[]{:S(2)}) collective-permute-start(f32[128,1024]{1,0:T(8,128)S(1)} %get-tuple-element.20.moved), channel_id=1, source_target_pairs={{1,0},{2,1},{3,2},{4,3},{5,4},{6,5},{7,6},{8,7},{9,8},{10,9},{11,1... | collective-permute-start | bytes 1572872 | tf_op jit(solution)/shard_map/ppermute | solution.py:316
  10.1 1.2 %collective-permute-start.1 = (f32[1,1024]{1,0:T(1,128)S(1)}, f32[1,1024]{1,0:T(1,128)S(1)}, u32[]{:S(2)}, u32[]{:S(2)}) collective-permute-start(f32[1,1024]{1,0:T(1,128)S(1)} %copy-done), channel_id=1, source_target_pairs={{0,1},{1,2},{2,3},{3,4},{4,5},{5,6},{6,7},{7,8},{8,9},{9,10},{10,1... | collective-permute-start | bytes 12296 | tf_op jit(solution)/shard_map/ppermute | solution.py:311
  18.4 4.9 %collective-permute-start.2 = (f32[136,512]{1,0:T(8,128)S(1)}, f32[136,512]{1,0:T(8,128)S(1)}, u32[]{:S(2)}, u32[]{:S(2)}) collective-permute-start(f32[136,512]{1,0:T(8,128)S(1)} %get-tuple-element.24), channel_id=1, source_target_pairs={{0,1},{1,0},{2,3},{3,2},{4,5},{5,4},{6,7},{7,6},{8,9},{9,8},{10,11... | collective-permute-start | bytes 835592 | tf_op jit(solution)/shard_map/ppermute | solution.py:311
  24.1 20.4 %all-to-all-start = ((f32[32,17,1,128]{3,2,1,0:T(1,128)}), f32[32,17,1,128]{3,2,1,0:T(1,128)S(1)}, u32[]{:S(2)}, u32[]{:S(2)}) async-start(f32[32,17,1,128]{3,2,1,0:T(1,128)} %bitcast), calls=%async_computation | async-start | bytes 557056 | tf_op jit(solution)/shard_map/all_to_all | solution.py:381
  34.2 17.2 %collective-permute-start.6 = (f32[128,1024]{1,0:T(8,128)S(1)}, f32[128,1024]{1,0:T(8,128)S(1)}, u32[]{:S(2)}, u32[]{:S(2)}) collective-permute-start(f32[128,1024]{1,0:T(8,128)S(1)} %get-tuple-element.28), channel_id=1, source_target_pairs={{1,0},{2,1},{3,2},{4,3},{5,4},{6,5},{7,6},{8,7},{9,8},{10,9},{11,1... | collective-permute-start | bytes 1572872 | tf_op jit(solution)/shard_map/ppermute | solution.py:316
  36.6 14.9 %collective-permute-start.7 = (f32[128,512]{1,0:T(8,128)S(1)}, f32[128,512]{1,0:T(8,128)S(1)}, u32[]{:S(2)}, u32[]{:S(2)}) collective-permute-start(f32[128,512]{1,0:T(8,128)S(1)} %get-tuple-element.29), channel_id=1, source_target_pairs={{0,1},{1,0},{2,3},{3,2},{4,5},{5,4},{6,7},{7,6},{8,9},{9,8},{10,11... | collective-permute-start | bytes 786440 | tf_op jit(solution)/shard_map/ppermute | solution.py:311
  44.6 6.9 %collective-permute-start.5 = (f32[24,128]{1,0:T(8,128)S(1)}, f32[24,128]{1,0:T(8,128)S(1)}, u32[]{:S(2)}, u32[]{:S(2)}) collective-permute-start(f32[24,128]{1,0:T(8,128)S(1)} %get-tuple-element.27.after), channel_id=1, source_target_pairs={{0,64},{64,128},{128,192},{192,0},{1,65},{65,129},{129,193},{193,1... | collective-permute-start | bytes 36872 | tf_op jit(solution)/shard_map/ppermute | solution.py:311
  45.9 5.6 %collective-permute-start.4 = (f32[24,128]{1,0:T(8,128)S(1)}, f32[24,128]{1,0:T(8,128)S(1)}, u32[]{:S(2)}, u32[]{:S(2)}) collective-permute-start(f32[24,128]{1,0:T(8,128)S(1)} %get-tuple-element.27.after), channel_id=1, source_target_pairs={{0,128},{64,192},{128,0},{192,64},{1,129},{65,193},{129,1},{193,65... | collective-permute-start | bytes 36872 | tf_op jit(solution)/shard_map/ppermute | solution.py:311
  47.5 4.0 %collective-permute-start.3 = (f32[24,128]{1,0:T(8,128)S(1)}, f32[24,128]{1,0:T(8,128)S(1)}, u32[]{:S(2)}, u32[]{:S(2)}) collective-permute-start(f32[24,128]{1,0:T(8,128)S(1)} %get-tuple-element.27.after), channel_id=1, source_target_pairs={{0,192},{64,0},{128,64},{192,128},{1,193},{65,1},{129,65},{193,129... | collective-permute-start | bytes 36872 | tf_op jit(solution)/shard_map/ppermute | solution.py:311
  67.7 4.8 %collective-permute-start.8 = (f32[32,16,128]{2,1,0:T(8,128)S(1)}, f32[32,16,128]{2,1,0:T(8,128)S(1)}, u32[]{:S(2)}, u32[]{:S(2)}) collective-permute-start(f32[32,16,128]{2,1,0:T(8,128)S(1)} %all_to_all.10.q_own), channel_id=1, source_target_pairs={{0,1},{1,0},{2,3},{3,2},{4,5},{5,4},{6,7},{7,6},{8,9},{9,8},{10,11... | collective-permute-start | bytes 786440 | tf_op jit(solution)/shard_map/ppermute | solution.py:311
